TPU v7x, 512 devices: a whole 4x4x16 slice. The times are simulated.
512 devices in a mesh: vox: 16 (over y, z_hi), feat: 32 (over x, z_lo, core).
Axes of the slice: x: 4, y: 4, z: 16 (z_hi: 4, z_lo: 4; z = z_hi * 4 + z_lo), core: 2. Of those that a mesh axis runs over, the one named last changes fastest.
Arguments:
- hidden_states: bfloat16 [8192, 8192], P('vox', 'feat'), may hold values from -6 to 6
- measured_signals: bfloat16 [8192, 2048], P('feat', 'vox'), may hold values from -6 to 6
- spectral_directions: bfloat16 [8192, 8192], P('feat'), may hold values from -0.0625 to 0.0625
- spectral_strengths: float32 [8192], replicated, may hold values from 0.002 to 0.02
- shrinkage_strengths: float32 [16], replicated, may hold values from 0.001 to 0.01
- chosen_shrinkage_slot: int32 [2048], P('vox'), may hold values from 0 to 15
Outputs:
- encoding: float32 [8192, 2048], P('feat', 'vox')
All inputs are finite; a program needn't handle non-finite values.
Results may differ from a plain program's by a relative error of at most 0.0036.
Values may be sent and summed in bfloat16 or wider, within the bound.
No kernel may reach another device: no remote copies, remote signals or barrier semaphores. Data moves between devices by JAX's collectives and lax.ppermute only.
A program may use at most 64 MiB of HBM per device.

v0:
```python
import jax
import jax.numpy as jnp
from jax import lax
from jax.sharding import PartitionSpec as P


def transposed_dot(left, right):
    return lax.dot_general(
        left, right, (((0,), (0,)), ((), ())), preferred_element_type=jnp.float32
    )


def per_device(
    hidden_states,
    measured_signals,
    spectral_directions,
    spectral_strengths,
    shrinkage_strengths,
    chosen_shrinkage_slot,
):
    feature_rows = lax.all_gather(hidden_states, "vox", axis=0, tiled=True)
    total_time = feature_rows.shape[0]
    cross = transposed_dot(
        feature_rows, lax.all_gather(measured_signals, "feat", axis=0, tiled=True)
    )
    covariance = (cross / total_time).astype(jnp.bfloat16)
    shrinkage_slots = jnp.arange(shrinkage_strengths.shape[0], dtype=jnp.int32)
    selection_mask = (chosen_shrinkage_slot[:, None] == shrinkage_slots[None, :]).astype(
        jnp.float32
    )
    fitted_coefficients = jnp.sum(selection_mask * shrinkage_strengths[None, :], axis=1)
    running_sum = transposed_dot(spectral_directions, covariance)
    eigen_rotated = lax.psum(running_sum, "feat")
    shrunk = (eigen_rotated / (spectral_strengths[:, None] + fitted_coefficients[None, :])).astype(
        jnp.bfloat16
    )
    encoding = jnp.dot(spectral_directions, shrunk, preferred_element_type=jnp.float32)
    return encoding


def solution(mesh):
    return jax.shard_map(
        per_device,
        mesh=mesh,
        in_specs=(P("vox", "feat"), P("feat", "vox"), P("feat", None), P(), P(), P("vox")),
        out_specs=P("feat", "vox"),
        check_vma=False,
    )
```

profile of v0, /device:TPU:1, one launch (start us, length us, event | category | flops | bytes accessed | tf_op | source)
XLA Modules:
  0.0 534.2 jit_solution(12345444218757080642)
XLA Ops:
  6.5 0.0 all-gather.5.cloned.1.call-start
  6.5 0.7 all-gather.5.cloned.1.call-update
  7.3 0.0 all-gather.3.cloned.1.call-start
  7.3 0.7 all-gather.3.cloned.1.call-update
  8.0 0.0 all-reduce.2.cloned.1.call-start
  8.1 72.5 %all-gather.5.cloned.1.call-done = bf16[8192,128]{1,0:T(8,128)(2,1)} async-done(((bf16[256,128]{1,0:T(8,128)(2,1)}), bf16[8192,128]{1,0:T(8,128)(2,1)}) %all-gather.5.cloned.1.call-update) | async-done | bytes 2097168 | tf_op jit(solution)/shard_map/all_gather | solution.py:24
  80.5 135.0 %all-gather.3.cloned.1.call-done = bf16[8192,256]{1,0:T(8,128)(2,1)} async-done(((bf16[512,256]{1,0:T(8,128)(2,1)}), bf16[8192,256]{1,0:T(8,128)(2,1)}) %all-gather.3.cloned.1.call-update) | async-done | bytes 4194320 | tf_op jit(solution)/shard_map/all_gather | solution.py:21
  215.6 8.0 %convolution_bitcast_fusion = f32[8192,128]{0,1:T(8,128)} fusion(bf16[256,8192]{1,0:T(8,128)(2,1)} %param.8, bf16[8192,256]{1,0:T(8,128)(2,1)} %all-gather.3.cloned.1.call-done, bf16[8192,128]{1,0:T(8,128)(2,1)} %all-gather.5.cloned.1.call-done), kind=kOutput, calls=%fused_computation | convolution fusion | flops 1073807360 | bytes 14680064 | tf_op jit(solution)/shard_map/dot_general | solution.py:8
  223.6 0.0 copy-start.1
  223.6 0.0 copy-start.2
  223.6 0.0 copy-start
  223.6 0.0 all-reduce.2.cloned.1.call-update
  223.6 0.6 copy-done.1
  224.2 0.0 copy-done.2
  224.2 0.1 select_reduce_fusion
  224.3 297.5 %all-reduce.2.cloned.1.call-done = f32[8192,128]{0,1:T(8,128)} async-done(((f32[8192,128]{0,1:T(8,128)}), f32[8192,128]{0,1:T(8,128)}) %all-reduce.2.cloned.1.call-update) | async-done | bytes 4194320 | tf_op jit(solution)/shard_map/psum | solution.py:33
  521.9 0.0 copy-done
  521.9 5.0 fusion.1
  526.9 0.8 copy.8
Async XLA Ops:
  6.5 74.0 %all-gather.5.cloned.1.call-start = ((), (), s32[]{:S(2)}) async-start(), calls=%async_computation.1 | async-start | bytes 2162688 | tf_op jit(solution)/shard_map/all_gather | solution.py:24
  7.3 208.3 %all-gather.3.cloned.1.call-start = ((), (), s32[]{:S(2)}) async-start(), calls=%async_computation | async-start | bytes 4456448 | tf_op jit(solution)/shard_map/all_gather | solution.py:21
  8.0 513.9 %all-reduce.2.cloned.1.call-start = ((), (), s32[]{:S(2)}) async-start(), calls=%async_computation.2 | async-start | bytes 8388608 | tf_op jit(solution)/shard_map/psum | solution.py:33
  223.6 0.7 copy-start.1
  223.6 0.7 copy-start.2
  223.6 298.3 %copy-start = (f32[8192]{0:T(1024)S(1)}, f32[8192]{0:T(1024)}, u32[]{:S(2)}) copy-start(f32[8192]{0:T(1024)} %param.9) | copy-start | bytes 98308
Sparse Core Ops, SparseCore 0:
  9.5 70.9 all-gather.4
  83.5 131.9 all-gather.2
  223.7 298.1 all-reduce.1
where the time goes:
time: 534 us
  waiting for transfers between devices  506 us (95%)
  between operations  13.1 us (2%)
  matrix products  13 us (2%)
    psum x1, waiting for transfers between devices, per_device(): eigen_rotated = lax.psum(running_sum, 'feat')  298 us
    all_gather x1, waiting for transfers between devices, per_device(): feature_rows = lax.all_gather(hidden_states, 'vox', axis=0, tiled=True)  135 us
    all_gather x1, waiting for transfers between devices, per_device(): lax.all_gather(measured_signals, 'feat', axis=0, tiled=True)  72.5 us
  transfers between devices with their start and end apart: 3, of which 3 were waited for; matrix products, arithmetic and copies ran while one was open for 0% of the time, Pallas kernels for 0%

commit v1 on v0

v1 whole, which is shorter than its diff:
```python
import jax
import jax.numpy as jnp
from jax import lax
from jax.sharding import Mesh, PartitionSpec as P


def exchange(blocks, axis):
    return lax.all_to_all(blocks, axis, 0, 0, tiled=True)


def gather(block, axis, size):
    blocks = jnp.broadcast_to(block[None], (size,) + block.shape)
    return exchange(blocks, axis)


def per_device(
    hidden_states,
    measured_signals,
    spectral_directions,
    spectral_strengths,
    shrinkage_strengths,
    chosen_shrinkage_slot,
):
    f32, bf16 = jnp.float32, jnp.bfloat16
    ny, nzh, nx, nzl, nc = (lax.axis_size(a) for a in ("y", "zh", "x", "zl", "core"))
    rows, width = spectral_directions.shape
    total_time = hidden_states.shape[0] * ny * nzh
    block, voxels = measured_signals.shape

    features = lax.all_gather(hidden_states, "y", axis=0, tiled=False)

    swap = [(a * nzl + b, b * nzl + a) for a in range(nzh) for b in range(nzl)]
    signals = lax.ppermute(measured_signals, ("zh", "zl"), swap)
    signals = gather(signals, "zl", nzl)
    signals = gather(signals, "x", nx)
    signals = gather(signals, "core", nc)

    features = features.reshape(ny, nc, block, rows)
    cross = jnp.einsum("ycta,cygtv->gav", features, signals, preferred_element_type=f32)
    cross = jnp.sum(
        exchange(cross.reshape(nzh, rows, voxels), "zh").reshape(nzh, rows, voxels), axis=0
    )
    covariance = (cross / total_time).astype(bf16)

    slots = jnp.arange(shrinkage_strengths.shape[0], dtype=jnp.int32)
    mask = (chosen_shrinkage_slot[:, None] == slots[None, :]).astype(f32)
    ridge = jnp.sum(mask * shrinkage_strengths[None, :], axis=1)

    rotated = lax.dot_general(
        covariance, spectral_directions, (((0,), (0,)), ((), ())), preferred_element_type=f32
    )
    rotated = rotated.reshape(voxels, nc, width // nc)
    core = lax.axis_index("core")
    mine = lax.dynamic_index_in_dim(rotated, core, 1, keepdims=False)
    other = lax.dynamic_index_in_dim(rotated, 1 - core, 1, keepdims=False)
    rotated = mine + lax.ppermute(other, "core", [(0, 1), (1, 0)])

    def scatter(values, axis, size):
        parts = values.astype(bf16).reshape(voxels, size, values.shape[1] // size)
        parts = exchange(parts.transpose(1, 0, 2), axis)
        return jnp.sum(parts.astype(f32), axis=0)

    rotated = scatter(rotated, "x", nx)
    rotated = scatter(rotated, "zl", nzl)
    share = rotated.shape[1]
    index = (core * nx + lax.axis_index("x")) * nzl + lax.axis_index("zl")
    strengths = lax.dynamic_slice_in_dim(spectral_strengths, index * share, share)
    shrunk = (rotated / (strengths[None, :] + ridge[:, None])).astype(bf16).T

    shrunk = gather(shrunk, "zl", nzl)
    shrunk = gather(shrunk, "x", nx)
    shrunk = gather(shrunk, "core", nc)
    shrunk = shrunk.reshape(width, voxels)
    return jnp.dot(spectral_directions, shrunk, preferred_element_type=f32)


def solution(mesh):
    fine = Mesh(mesh.devices.reshape(4, 4, 4, 4, 2), ("y", "zh", "x", "zl", "core"))
    vox, feat = ("y", "zh"), ("x", "zl", "core")
    return jax.shard_map(
        per_device,
        mesh=fine,
        in_specs=(P(vox, feat), P(feat, vox), P(feat, None), P(), P(), P(vox)),
        out_specs=P(feat, vox),
        check_vma=False,
    )
```

time: 534 us -> 220 us (0.41)
  waiting for transfers between devices: 506 us -> 44.3 us
  blocking collectives: 0 us -> 71.4 us
  starting transfers between devices: 0.08 us -> 45.9 us
  local copies, waits for them, and re-layouts: 1.4 us -> 31.8 us
    psum x1 -> x0, waiting for transfers between devices: 298 us -> none  [per_device(): eigen_rotated = lax.psum(running_sum, 'feat')]
    all_gather x2 -> x1, waiting for transfers between devices: 208 us -> 1.82 us  [per_device(): features = lax.all_gather(hidden_states, 'y', axis=0, tiled=False)]
    all_to_all x0 -> x5, blocking collectives: none -> 71.4 us  [exchange(): return lax.all_to_all(blocks, axis, 0, 0, tiled=True)]
    all_to_all x0 -> x4, starting transfers between devices: none -> 41.9 us  [exchange(): return lax.all_to_all(blocks, axis, 0, 0, tiled=True)]
    all_to_all x0 -> x4, waiting for transfers between devices: none -> 41.4 us  [exchange(): return lax.all_to_all(blocks, axis, 0, 0, tiled=True)]
    dynamic_slice x0 -> x4, local copies, waits for them, and re-layouts: none -> 19.4 us  [the longest x2 13 us: per_device(): mine = lax.dynamic_index_in_dim(rotated, core, 1, keepdims=False)]
    reshape x0 -> x1, local copies, waits for them, and re-layouts: none -> 6.57 us  [per_device(): rotated = rotated.reshape(voxels, nc, width // nc)]
    dot_general x2 -> x3, matrix products: 13 us -> 9.12 us  [the longest x1 4.89 us: per_device(): lax.dot_general(covariance, spectral_directions, (((0,), (0,)), ((), ()))...]
  transfers between devices with their start and end apart: 3 -> 7, of which waited for: 3 -> 6; matrix products, arithmetic and copies ran while one was open for 0% -> 3% of each run, Pallas kernels for 0% -> 0%
where the time goes in v1:
time: 220 us; the launch traced here: 219 us
  blocking collectives  71.4 us (32%)
  starting transfers between devices  45.9 us (21%)
  waiting for transfers between devices  44.3 us (20%)
  local copies, waits for them, and re-layouts  31.8 us (14%)
  between operations  13.5 us (6%)
  matrix products  9.12 us (4%)
  other arithmetic  2.87 us (1%)
    all_to_all x5, blocking collectives, exchange(): return lax.all_to_all(blocks, axis, 0, 0, tiled=True)  71.4 us
    all_to_all x4, starting transfers between devices, exchange(): return lax.all_to_all(blocks, axis, 0, 0, tiled=True)  41.9 us
    all_to_all x4, waiting for transfers between devices, exchange(): return lax.all_to_all(blocks, axis, 0, 0, tiled=True)  41.4 us
    dynamic_slice x2, local copies, waits for them, and re-layouts, per_device(): mine = lax.dynamic_index_in_dim(rotated, core, 1, keepdims=False)  13 us
    reshape x1, local copies, waits for them, and re-layouts, per_device(): rotated = rotated.reshape(voxels, nc, width // nc)  6.57 us
    dynamic_slice x1, local copies, waits for them, and re-layouts, per_device(): other = lax.dynamic_index_in_dim(rotated, 1 - core, 1, keepdims=False)  5.63 us
    dot_general x1, matrix products, per_device(): lax.dot_general(covariance, spectral_directions, (((0,), (0,)), ((), ()))...  4.89 us
  transfers between devices with their start and end apart: 7, of which 6 were waited for; matrix products, arithmetic and copies ran while one was open for 3% of the time, Pallas kernels for 0%

profile of v1, /device:TPU:1, one launch (start us, length us, event | category | flops | bytes accessed | tf_op | source)
XLA Modules:
  0.0 218.9 jit_solution(7263860966893981230)
XLA Ops:
  6.5 1.5 collective-permute-start
  8.0 0.0 collective-permute-done
  8.0 0.1 copy.35
  8.1 0.7 broadcast_in_dim.12
  8.9 20.1 %all-to-all-start = ((bf16[4,256,128]{1,2,0:T(8,128)(2,1)}), bf16[4,256,128]{1,2,0:T(8,128)(2,1)S(1)}, u32[]{:S(2)}, u32[]{:S(2)}) async-start(bf16[4,256,128]{1,2,0:T(8,128)(2,1)} %broadcast_in_dim.12), calls=%async_computation | async-start | bytes 524288 | tf_op jit(solution)/shard_map/all_to_all | solution.py:8
  28.9 0.0 all-gather.3.cloned.1.call-start
  28.9 0.7 all-gather.3.cloned.1.call-update
  29.6 6.8 %all-to-all-done = bf16[4,256,128]{1,2,0:T(8,128)(2,1)S(1)} async-done(((bf16[4,256,128]{1,2,0:T(8,128)(2,1)}), bf16[4,256,128]{1,2,0:T(8,128)(2,1)S(1)}, u32[]{:S(2)}, u32[]{:S(2)}) %all-to-all-start) | async-done | bytes 262176 | tf_op jit(solution)/shard_map/all_to_all | solution.py:8
  36.5 0.1 broadcast_in_dim.13
  36.6 16.4 %all_to_all.45 = bf16[4,4,256,128]{2,3,1,0:T(8,128)(2,1)S(1)} all-to-all(bf16[4,4,256,128]{2,3,1,0:T(8,128)(2,1)S(1)} %broadcast_in_dim.13), channel_id=1, replica_groups=mesh['y'=4,'zh'=4,'x'=4,'zl'=4,'core'=2] {'x'}, dimensions={0} | all-to-all | bytes 2097152 | tf_op jit(solution)/shard_map/all_to_all | solution.py:8
  53.0 1.6 broadcast_in_dim.14
  54.6 7.2 %all-to-all-start.2 = ((bf16[2,4,4,256,128]{3,4,2,1,0:T(8,128)(2,1)}), bf16[2,4,4,256,128]{3,4,2,1,0:T(8,128)(2,1)S(1)}, u32[]{:S(2)}, u32[]{:S(2)}) async-start(bf16[2,4,4,256,128]{3,4,2,1,0:T(8,128)(2,1)} %broadcast_in_dim.14), calls=%async_computation.2 | async-start | bytes 4194304 | tf_op jit(solution)/shard_map/all_to_all | solution.py:8
  61.8 1.8 all-gather.3.cloned.1.call-done
  63.6 0.7 all-to-all-done.2
  64.3 2.7 %convolution_bitcast_fusion = f32[4,256,128]{1,2,0:T(8,128)} fusion(bf16[2,4,4,256,128]{3,4,2,1,0:T(8,128)(2,1)S(1)} %all-to-all-done.2, bf16[4,2,256,256,1]{3,2,1,0,4:T(8,128)(2,1)} %bitcast.35), kind=kOutput, calls=%fused_computation.2 | convolution fusion | flops 536870912 | bytes 3670016 | tf_op jit(solution)/shard_map/ycta,cygtv->gav/dot_general | solution.py:39
  67.0 11.2 %all-to-all-start.3 = ((f32[4,256,128]{1,2,0:T(8,128)}), f32[4,256,128]{1,2,0:T(8,128)S(1)}, u32[]{:S(2)}, u32[]{:S(2)}) async-start(f32[4,256,128]{1,2,0:T(8,128)} %convolution_bitcast_fusion), calls=%async_computation.3 | async-start | bytes 1048576 | tf_op jit(solution)/shard_map/all_to_all | solution.py:8
  78.2 29.1 %all-to-all-done.3 = f32[4,256,128]{1,2,0:T(8,128)S(1)} async-done(((f32[4,256,128]{1,2,0:T(8,128)}), f32[4,256,128]{1,2,0:T(8,128)S(1)}, u32[]{:S(2)}, u32[]{:S(2)}) %all-to-all-start.3) | async-done | bytes 524320 | tf_op jit(solution)/shard_map/all_to_all | solution.py:8
  107.4 4.9 %fusion.3 = f32[128,8192]{1,0:T(8,128)} fusion(bf16[256,8192]{1,0:T(8,128)(2,1)} %param.8, f32[256,128]{0,1:T(8,128)S(1)} %reduce_sum.41), kind=kOutput, calls=%fused_computation.9 | convolution fusion | flops 536936448 | bytes 8519680 | tf_op jit(solution)/shard_map/dot_general | solution.py:49
  112.2 6.6 %reshape.26 = f32[128,2,4096]{2,1,0:T(2,128)} reshape(f32[128,8192]{1,0:T(8,128)} %fusion.3) | data formatting | bytes 8388608 | tf_op jit(solution)/shard_map/reshape | solution.py:52
  118.8 9.2 %constant_dynamic-slice_fusion.1 = (f32[128,1,4096]{2,1,0:T(1,128)S(1)}, f32[128,1,4096]{2,1,0:T(1,128)}) fusion(f32[128,2,4096]{2,1,0:T(2,128)} %reshape.26, s32[]{:T(128)S(6)} %select_n.10, s32[]{:T(128)S(6)} %select_n.11), kind=kLoop, calls=%fused_computation.14 | loop fusion | bytes 8388616 | tf_op jit(solution)/shard_map/jit(dynamic_index_in_dim)/dynamic_slice | solution.py:54
  128.1 5.6 %copy.38 = f32[128,1,4096]{0,2,1:T(8,128)} copy(f32[128,1,4096]{2,1,0:T(1,128)} %get-tuple-element.6) | data formatting | bytes 4194304 | tf_op jit(solution)/shard_map/jit(dynamic_index_in_dim)/dynamic_slice | solution.py:55
  133.7 2.5 %collective-permute-start.1 = (f32[128,4096]{0,1:T(8,128)}, f32[128,4096]{0,1:T(8,128)}, u32[]{:S(2)}, u32[]{:S(2)}) collective-permute-start(f32[128,4096]{0,1:T(8,128)} %bitcast.33), channel_id=1, source_target_pairs={{0,1},{1,0},{2,3},{3,2},{4,5},{5,4},{6,7},{7,6},{8,9},{9,8},{10,11... | collective-permute-start | bytes 6291464 | tf_op jit(solution)/shard_map/ppermute | solution.py:56
  136.2 3.8 %copy.37 = f32[128,1,4096]{0,2,1:T(8,128)} copy(f32[128,1,4096]{2,1,0:T(1,128)S(1)} %get-tuple-element.5) | data formatting | bytes 4194304 | tf_op jit(solution)/shard_map/jit(dynamic_index_in_dim)/dynamic_slice | solution.py:54
  140.0 0.3 collective-permute-done.1
  140.3 2.4 %fusion = bf16[128,4096]{0,1:T(8,128)(2,1)S(1)} fusion(f32[128,4096]{0,1:T(8,128)} %collective-permute-done.1, f32[128,1,4096]{0,2,1:T(8,128)} %copy.37), kind=kLoop, calls=%fused_computation.1 | loop fusion | flops 1048576 | bytes 5242880 | tf_op jit(solution)/shard_map/convert_element_type | solution.py:59
  142.7 0.5 copy.39
  143.3 0.0 copy-start.1
  143.3 0.0 copy-start.2
  143.3 20.5 %all_to_all.46 = bf16[4,128,1024]{2,1,0:T(8,128)(2,1)S(1)} all-to-all(bf16[4,128,1024]{2,1,0:T(8,128)(2,1)S(1)} %copy.39), channel_id=1, replica_groups=mesh['y'=4,'zh'=4,'x'=4,'zl'=4,'core'=2] {'x'}, dimensions={0} | all-to-all | bytes 2097152 | tf_op jit(solution)/shard_map/all_to_all | solution.py:8
  163.8 0.2 reduce_sum.42
  164.0 0.2 copy.40
  164.1 0.9 copy.41
  165.0 3.4 %all-to-all-start.5 = ((bf16[4,128,256]{2,1,0:T(8,128)(2,1)}), bf16[4,128,256]{2,1,0:T(8,128)(2,1)S(1)}, u32[]{:S(2)}, u32[]{:S(2)}) async-start(bf16[4,128,256]{2,1,0:T(8,128)(2,1)} %copy.41), calls=%async_computation.5 | async-start | bytes 524288 | tf_op jit(solution)/shard_map/all_to_all | solution.py:8
  168.4 0.8 dynamic_slice.12
  169.2 0.0 copy-done.1
  169.2 0.0 copy-done.2
  169.2 0.1 select_reduce_fusion
  169.3 4.8 %all-to-all-done.5 = bf16[4,128,256]{2,1,0:T(8,128)(2,1)S(1)} async-done(((bf16[4,128,256]{2,1,0:T(8,128)(2,1)}), bf16[4,128,256]{2,1,0:T(8,128)(2,1)S(1)}, u32[]{:S(2)}, u32[]{:S(2)}) %all-to-all-start.5) | async-done | bytes 262176 | tf_op jit(solution)/shard_map/all_to_all | solution.py:8
  174.1 0.1 fusion.2
  174.2 0.1 copy.42
  174.4 10.8 %all_to_all.47 = bf16[4,256,128]{2,1,0:T(8,128)(2,1)S(1)} all-to-all(bf16[4,256,128]{2,1,0:T(8,128)(2,1)S(1)} %broadcast_in_dim.15), channel_id=1, replica_groups=mesh['y'=4,'zh'=4,'x'=4,'zl'=4,'core'=2] {'zl'}, dimensions={0} | all-to-all | bytes 524288 | tf_op jit(solution)/shard_map/all_to_all | solution.py:8
  185.1 0.2 broadcast_in_dim.16
  185.3 13.8 %all_to_all.48 = bf16[4,4,256,128]{3,2,1,0:T(8,128)(2,1)S(1)} all-to-all(bf16[4,4,256,128]{3,2,1,0:T(8,128)(2,1)S(1)} %broadcast_in_dim.16), channel_id=1, replica_groups=mesh['y'=4,'zh'=4,'x'=4,'zl'=4,'core'=2] {'x'}, dimensions={0} | all-to-all | bytes 2097152 | tf_op jit(solution)/shard_map/all_to_all | solution.py:8
  199.1 0.6 broadcast_in_dim.17
  199.7 0.0 copy-start
  199.7 10.0 %all_to_all.49 = bf16[2,4,4,256,128]{4,3,2,1,0:T(8,128)(2,1)S(1)} all-to-all(bf16[2,4,4,256,128]{4,3,2,1,0:T(8,128)(2,1)S(1)} %broadcast_in_dim.17), channel_id=1, replica_groups=mesh['y'=4,'zh'=4,'x'=4,'zl'=4,'core'=2] {'core'}, dimensions={0} | all-to-all | bytes 4194304 | tf_op jit(solution)/shard_map/all_to_all | solution.py:8
  209.7 0.0 copy-done
  209.7 1.5 convolution_bitcast_fusion.1
  211.3 0.8 copy.43
  (3 shorter events, 0.1 us)
Async XLA Ops:
  6.5 1.5 collective-permute-start
  8.9 27.6 %all-to-all-start = ((bf16[4,256,128]{1,2,0:T(8,128)(2,1)}), bf16[4,256,128]{1,2,0:T(8,128)(2,1)S(1)}, u32[]{:S(2)}, u32[]{:S(2)}) async-start(bf16[4,256,128]{1,2,0:T(8,128)(2,1)} %broadcast_in_dim.12), calls=%async_computation | async-start | bytes 524288 | tf_op jit(solution)/shard_map/all_to_all | solution.py:8
  28.9 34.7 %all-gather.3.cloned.1.call-start = ((), (), s32[]{:S(2)}) async-start(), calls=%async_computation.9 | async-start | bytes 1310720 | tf_op jit(solution)/shard_map/all_gather | solution.py:30
  54.6 9.7 %all-to-all-start.2 = ((bf16[2,4,4,256,128]{3,4,2,1,0:T(8,128)(2,1)}), bf16[2,4,4,256,128]{3,4,2,1,0:T(8,128)(2,1)S(1)}, u32[]{:S(2)}, u32[]{:S(2)}) async-start(bf16[2,4,4,256,128]{3,4,2,1,0:T(8,128)(2,1)} %broadcast_in_dim.14), calls=%async_computation.2 | async-start | bytes 4194304 | tf_op jit(solution)/shard_map/all_to_all | solution.py:8
  67.0 40.3 %all-to-all-start.3 = ((f32[4,256,128]{1,2,0:T(8,128)}), f32[4,256,128]{1,2,0:T(8,128)S(1)}, u32[]{:S(2)}, u32[]{:S(2)}) async-start(f32[4,256,128]{1,2,0:T(8,128)} %convolution_bitcast_fusion), calls=%async_computation.3 | async-start | bytes 1048576 | tf_op jit(solution)/shard_map/all_to_all | solution.py:8
  133.7 6.6 %collective-permute-start.1 = (f32[128,4096]{0,1:T(8,128)}, f32[128,4096]{0,1:T(8,128)}, u32[]{:S(2)}, u32[]{:S(2)}) collective-permute-start(f32[128,4096]{0,1:T(8,128)} %bitcast.33), channel_id=1, source_target_pairs={{0,1},{1,0},{2,3},{3,2},{4,5},{5,4},{6,7},{7,6},{8,9},{9,8},{10,11... | collective-permute-start | bytes 6291464 | tf_op jit(solution)/shard_map/ppermute | solution.py:56
  143.3 25.9 %copy-start.1 = (f32[16]{0:T(128)S(1)}, f32[16]{0:T(128)}, u32[]{:S(2)}) copy-start(f32[16]{0:T(128)} %param.10) | copy-start | bytes 196
  143.3 25.9 %copy-start.2 = (s32[128]{0:T(128)S(1)}, s32[128]{0:T(128)}, u32[]{:S(2)}) copy-start(s32[128]{0:T(128)} %param.11) | copy-start | bytes 1540
  165.0 9.1 %all-to-all-start.5 = ((bf16[4,128,256]{2,1,0:T(8,128)(2,1)}), bf16[4,128,256]{2,1,0:T(8,128)(2,1)S(1)}, u32[]{:S(2)}, u32[]{:S(2)}) async-start(bf16[4,128,256]{2,1,0:T(8,128)(2,1)} %copy.41), calls=%async_computation.5 | async-start | bytes 524288 | tf_op jit(solution)/shard_map/all_to_all | solution.py:8
  199.7 10.0 %copy-start = (bf16[256,8192]{1,0:T(8,128)(2,1)S(1)}, bf16[256,8192]{1,0:T(8,128)(2,1)}, u32[]{:S(2)}) copy-start(bf16[256,8192]{1,0:T(8,128)(2,1)} %param.8) | copy-start | bytes 12582916
Sparse Core Ops, SparseCore 0:
  31.8 31.7 all-gather.2

commit v2 on v0

v2 whole, which is shorter than its diff:
```python
import functools

import jax
import jax.numpy as jnp
from jax import lax
from jax.experimental import pallas as pl
from jax.experimental.pallas import tpu as pltpu
from jax.sharding import Mesh, PartitionSpec as P

F32, BF16, F16 = jnp.float32, jnp.bfloat16, jnp.float16
STEPS = (64, 32, 16, 8, 4, 2, 1)
EXTRA = 16


def exchange(blocks, axis):
    return lax.all_to_all(blocks, axis, 0, 0, tiled=True)


def gather(block, axis, size):
    return exchange(jnp.broadcast_to(block[None], (size,) + block.shape), axis)


def shift(block, axis, size, by):
    return lax.ppermute(block, axis, [(i, (i + by) % size) for i in range(size)])


def whole(count):
    return [pl.BlockSpec(memory_space=pltpu.VMEM)] * count


def cross_kernel(ny, block, first, where, *refs):
    features, signals, total, out = refs[:ny], refs[ny], refs[-2], refs[-1]
    start = pl.multiple_of(where[1] * block, block)
    groups, voxels, _ = signals.shape[1:]
    acc = None if first else total[...]
    for k in range(ny):
        other = lax.rem(where[0] - k + ny, ny)
        left = signals[other].reshape(groups * voxels, block)
        right = features[k][pl.ds(start, block), :]
        term = jnp.dot(left, right, preferred_element_type=F32)
        acc = term if acc is None else acc + term
    if first:
        out[...] = acc
        return
    acc = acc * (1.0 / (ny * groups * 2 * block))
    top = jnp.max(jnp.max(jnp.abs(acc), axis=0, keepdims=True), axis=1, keepdims=True)
    scale, exponent = jnp.ones_like(top), jnp.zeros_like(top)
    for step in STEPS:
        grown = scale * 2.0**step
        fits = top * grown < 2.0**14
        scale = jnp.where(fits, grown, scale)
        exponent = jnp.where(fits, exponent + step, exponent)
    out[:, :voxels, :] = (acc * scale).reshape(groups, voxels, -1)
    out[:, voxels:, :] = jnp.broadcast_to(exponent[None], (groups, EXTRA, acc.shape[1]))


def cross_products(where, features, signals, total):
    ny, (time, rows) = len(features), features[0].shape
    _, groups, voxels, block = signals.shape
    first = total is None
    operands = list(features) + [signals] + ([] if first else [total])
    shape = (groups * voxels, rows) if first else (groups, voxels + EXTRA, rows)
    return pl.pallas_call(
        functools.partial(cross_kernel, ny, block, first),
        out_shape=jax.ShapeDtypeStruct(shape, F32),
        in_specs=[pl.BlockSpec(memory_space=pltpu.SMEM)] + whole(len(operands)),
        out_specs=pl.BlockSpec(memory_space=pltpu.VMEM),
        compiler_params=pltpu.CompilerParams(vmem_limit_bytes=16 << 20),
        cost_estimate=pl.CostEstimate(
            flops=2 * ny * block * groups * voxels * rows, bytes_accessed=4 << 20, transcendentals=0
        ),
    )(where, *operands)


def covariance_kernel(parts, out):
    voxels = out.shape[0]
    total = None
    for k in range(parts.shape[0]):
        exponent = parts[k, voxels : voxels + 1, :]
        scale = jnp.ones_like(exponent)
        for step in STEPS:
            holds = exponent >= step
            scale = jnp.where(holds, scale * 0.5**step, scale)
            exponent = jnp.where(holds, exponent - step, exponent)
        term = parts[k, :voxels, :] * scale
        total = term if total is None else total + term
    out[...] = total.astype(out.dtype)


def rounded_covariance(parts):
    count, rows, width = parts.shape
    return pl.pallas_call(
        covariance_kernel,
        out_shape=jax.ShapeDtypeStruct((rows - EXTRA, width), BF16),
        in_specs=whole(1),
        out_specs=pl.BlockSpec(memory_space=pltpu.VMEM),
        compiler_params=pltpu.CompilerParams(vmem_limit_bytes=16 << 20),
        cost_estimate=pl.CostEstimate(
            flops=2 * parts.size, bytes_accessed=4 * parts.size, transcendentals=0
        ),
    )(parts)


def rotate_kernel(half, own, directions, theirs, their_directions, out):
    product = jnp.dot(own[...], directions[...], preferred_element_type=F32)
    product += jnp.dot(theirs[...], their_directions[...], preferred_element_type=F32)
    share = out.shape[-1]
    for j in range(out.shape[1]):
        out[0, j] = product[:, j * share : (j + 1) * share].astype(out.dtype)


def rotate(half, own, directions, theirs, their_directions, nx, nzl):
    voxels, rows = own.shape
    columns = their_directions.shape[1] // nx
    share = columns // nzl
    flat = pl.BlockSpec((voxels, rows), lambda i, h: (0, 0))
    return pl.pallas_call(
        rotate_kernel,
        out_shape=jax.ShapeDtypeStruct((nx, nzl, voxels, share), BF16),
        grid_spec=pltpu.PrefetchScalarGridSpec(
            num_scalar_prefetch=1,
            grid=(nx,),
            in_specs=[
                flat,
                pl.BlockSpec((rows, columns), lambda i, h: (0, h[0] * nx + i)),
                flat,
                pl.BlockSpec((rows, columns), lambda i, h: (0, i)),
            ],
            out_specs=pl.BlockSpec((1, nzl, voxels, share), lambda i, h: (i, 0, 0, 0)),
        ),
        compiler_params=pltpu.CompilerParams(vmem_limit_bytes=16 << 20),
        cost_estimate=pl.CostEstimate(
            flops=4 * rows * columns * nx * voxels, bytes_accessed=4 << 20, transcendentals=0
        ),
    )(half, own, directions, theirs, their_directions)


def add_kernel(parts, out):
    out[...] = jnp.sum(parts[...].astype(F32), axis=0).astype(out.dtype)


def add_parts(parts):
    return pl.pallas_call(
        add_kernel,
        out_shape=jax.ShapeDtypeStruct(parts.shape[1:], BF16),
        in_specs=whole(1),
        out_specs=pl.BlockSpec(memory_space=pltpu.VMEM),
        compiler_params=pltpu.CompilerParams(vmem_limit_bytes=16 << 20),
        cost_estimate=pl.CostEstimate(
            flops=parts.size, bytes_accessed=3 * parts.size, transcendentals=0
        ),
    )(parts)


def shrink_kernel(levels, which, parts, strengths, slots, grid_values, out):
    voxels = slots.shape[1]
    ridge = jnp.zeros((1, voxels), F32)
    for level in range(levels):
        ridge = jnp.where(slots[...] == level, grid_values[level], ridge)
    column = jnp.broadcast_to(ridge, (voxels, voxels)).T
    rotated = jnp.sum(parts[...].astype(F32), axis=0)
    for j in range(0, out.shape[0], voxels):
        denominator = strengths[0, :, j : j + voxels] + column
        out[j : j + voxels, :] = (rotated[:, j : j + voxels] / denominator).T.astype(out.dtype)


def shrink(which, parts, strengths, grid_values, slots):
    _, voxels, share = parts.shape
    levels = grid_values.shape[0]
    return pl.pallas_call(
        functools.partial(shrink_kernel, levels),
        out_shape=jax.ShapeDtypeStruct((share, voxels), BF16),
        grid_spec=pltpu.PrefetchScalarGridSpec(
            num_scalar_prefetch=1,
            grid=(1,),
            in_specs=[
                pl.BlockSpec(parts.shape, lambda i, w: (0, 0, 0)),
                pl.BlockSpec((1, 1, share), lambda i, w: (w[0], 0, 0)),
                pl.BlockSpec((1, voxels), lambda i, w: (0, 0)),
                pl.BlockSpec(memory_space=pltpu.SMEM),
            ],
            out_specs=pl.BlockSpec((share, voxels), lambda i, w: (0, 0)),
        ),
        compiler_params=pltpu.CompilerParams(vmem_limit_bytes=16 << 20),
        cost_estimate=pl.CostEstimate(
            flops=6 * parts.size, bytes_accessed=2 * parts.size, transcendentals=0
        ),
    )(which, parts, strengths.reshape(-1, 1, share), slots.reshape(1, voxels), grid_values)


def encode_kernel(half, directions, shrunk, out):
    @pl.when(pl.program_id(0) == 0)
    def _():
        out[...] = jnp.zeros_like(out)

    out[...] += jnp.dot(directions[...], shrunk[...], preferred_element_type=F32)


def encode(half, directions, shrunk, steps=4):
    rows, _ = directions.shape
    depth, voxels = shrunk.shape
    columns = depth // steps
    return pl.pallas_call(
        encode_kernel,
        out_shape=jax.ShapeDtypeStruct((rows, voxels), F32),
        grid_spec=pltpu.PrefetchScalarGridSpec(
            num_scalar_prefetch=1,
            grid=(steps,),
            in_specs=[
                pl.BlockSpec((rows, columns), lambda i, h: (0, h[0] * steps + i)),
                pl.BlockSpec((columns, voxels), lambda i, h: (i, 0)),
            ],
            out_specs=pl.BlockSpec((rows, voxels), lambda i, h: (0, 0)),
        ),
        compiler_params=pltpu.CompilerParams(vmem_limit_bytes=16 << 20),
        cost_estimate=pl.CostEstimate(
            flops=2 * rows * depth * voxels, bytes_accessed=4 << 20, transcendentals=0
        ),
    )(half, directions, shrunk)


def per_device(
    hidden_states,
    measured_signals,
    spectral_directions,
    spectral_strengths,
    shrinkage_strengths,
    chosen_shrinkage_slot,
):
    ny, nzh, nx, nzl = (lax.axis_size(a) for a in ("y", "zh", "x", "zl"))
    width = spectral_directions.shape[1]
    core = lax.axis_index("core")
    mine, other = core.reshape(1), (1 - core).reshape(1)
    y = lax.axis_index("y").reshape(1)

    swap = [(a * nzl + b, b * nzl + a) for a in range(nzh) for b in range(nzl)]
    signals = lax.ppermute(measured_signals.T, ("zh", "zl"), swap)
    given = lax.dynamic_slice_in_dim(spectral_directions, (1 - core) * (width // 2), width // 2, axis=1)
    features = [hidden_states] + [shift(hidden_states, "y", ny, k) for k in range(1, ny)]
    signals, given = lax.optimization_barrier((signals, given))
    signals = gather(signals, "zl", nzl)
    signals = gather(signals, "x", nx)
    signals, *features = lax.optimization_barrier((signals, *features))
    signals_other = shift(signals, "core", 2, 1)
    cross = cross_products(jnp.concatenate([y, mine]), features, signals, None)
    cross = cross_products(jnp.concatenate([y, other]), features, signals_other, cross)
    cross, given = lax.optimization_barrier((cross, given))
    their_directions = shift(given, "core", 2, 1)
    parts = exchange(cross.astype(F16), "zh").astype(F32)
    parts, their_directions = lax.optimization_barrier((parts, their_directions))

    covariance = rounded_covariance(parts)
    their_covariance = shift(covariance, "core", 2, 1)
    rotated = rotate(
        mine, covariance, spectral_directions, their_covariance, their_directions, nx, nzl
    )
    rotated = exchange(rotated, "x")
    rotated = exchange(add_parts(rotated), "zl")
    index = (core * nx + lax.axis_index("x")) * nzl + lax.axis_index("zl")
    shrunk = shrink(
        index.reshape(1), rotated, spectral_strengths, shrinkage_strengths, chosen_shrinkage_slot
    )

    shrunk = gather(shrunk, "zl", nzl)
    shrunk = gather(shrunk, "x", nx).reshape(width // 2, -1)
    theirs = encode(jnp.zeros((1,), jnp.int32), their_directions, shrunk)
    received = shift(theirs, "core", 2, 1)
    return encode(mine, spectral_directions, shrunk) + received


def solution(mesh):
    fine = Mesh(mesh.devices.reshape(4, 4, 4, 4, 2), ("y", "zh", "x", "zl", "core"))
    vox, feat = ("y", "zh"), ("x", "zl", "core")
    return jax.shard_map(
        per_device,
        mesh=fine,
        in_specs=(P(vox, feat), P(feat, vox), P(feat, None), P(), P(), P(vox)),
        out_specs=P(feat, vox),
        check_vma=False,
    )
```

time: 534 us -> 163 us (0.31)
  waiting for transfers between devices: 506 us -> 14.2 us
  blocking collectives: 0 us -> 91.5 us
  starting transfers between devices: 0.08 us -> 42.9 us
  matrix products: 13 us -> 0 us
  between operations: 13.1 us -> 0.25 us
  Pallas kernels: 0 us -> 8.12 us
    psum x1 -> x0, waiting for transfers between devices: 298 us -> none  [per_device(): eigen_rotated = lax.psum(running_sum, 'feat')]
    all_gather x2 -> x0, waiting for transfers between devices: 208 us -> none  [the longest x1 135 us: per_device(): feature_rows = lax.all_gather(hidden_states, 'vox', axis=0, tiled=True)]
    all_to_all x0 -> x5, blocking collectives: none -> 91.5 us  [exchange(): return lax.all_to_all(blocks, axis, 0, 0, tiled=True)]
    ppermute x0 -> x8, starting transfers between devices: none -> 32.4 us  [the longest x7 30.9 us: shift(): lax.ppermute(block, axis, [(i, (i + by) % size) for i in range(size)])]
    dot_general x2 -> x0, matrix products: 13 us -> none  [the longest x1 8.01 us: transposed_dot(): lax.dot_general(left, right, (((0,), (0,)), ((), ())), preferred_element_...]
    all_to_all x0 -> x2, starting transfers between devices: none -> 10.5 us  [exchange(): return lax.all_to_all(blocks, axis, 0, 0, tiled=True)]
    ppermute x0 -> x8, waiting for transfers between devices: none -> 8.53 us  [the longest x7 8.52 us: shift(): lax.ppermute(block, axis, [(i, (i + by) % size) for i in range(size)])]
    pallas_call x0 -> x8, Pallas kernels: none -> 8.12 us  [the longest x2 2.78 us: encode(): pl.pallas_call(encode_kernel, out_shape=jax.ShapeDtypeStruct((rows, voxel...]
  transfers between devices with their start and end apart: 3 -> 10, of which waited for: 3 -> 5; matrix products, arithmetic and copies ran while one was open for 0% -> 2% of each run, Pallas kernels for 0% -> 1%
where the time goes in v2:
time: 163 us; the launch traced here: 162 us
  blocking collectives  91.5 us (56%)
  starting transfers between devices  42.9 us (26%)
  waiting for transfers between devices  14.2 us (9%)
  Pallas kernels  8.12 us (5%)
  local copies, waits for them, and re-layouts  4.62 us (3%)
    all_to_all x5, blocking collectives, exchange(): return lax.all_to_all(blocks, axis, 0, 0, tiled=True)  91.5 us
    ppermute x7, starting transfers between devices, shift(): lax.ppermute(block, axis, [(i, (i + by) % size) for i in range(size)])  30.9 us
    all_to_all x2, starting transfers between devices, exchange(): return lax.all_to_all(blocks, axis, 0, 0, tiled=True)  10.5 us
    ppermute x7, waiting for transfers between devices, shift(): lax.ppermute(block, axis, [(i, (i + by) % size) for i in range(size)])  8.52 us
    all_to_all x2, waiting for transfers between devices, exchange(): return lax.all_to_all(blocks, axis, 0, 0, tiled=True)  5.68 us
  transfers between devices with their start and end apart: 10, of which 5 were waited for; matrix products, arithmetic and copies ran while one was open for 2% of the time, Pallas kernels for 1%

profile of v2, /device:TPU:1, one launch (start us, length us, event | category | flops | bytes accessed | tf_op | source)
XLA Modules:
  0.0 162.5 jit_solution(13884283584876631658)
XLA Ops:
  0.0 1.5 collective-permute-start
  1.5 3.1 %constant_dynamic-slice_fusion = bf16[256,4096]{1,0:T(8,128)(2,1)} fusion(bf16[256,8192]{1,0:T(8,128)(2,1)} %directions.3, s32[]{:T(128)S(6)} %select_n.3), kind=kLoop, calls=%fused_computation.2 | loop fusion | bytes 4194308 | tf_op jit(solution)/shard_map/dynamic_slice | solution.py:238
  4.6 0.0 collective-permute-done
  4.6 0.1 copy.7
  4.8 0.0 copy-start.2
  4.8 22.9 %all_to_all.35 = bf16[4,128,256]{2,1,0:T(8,128)(2,1)S(1)} all-to-all(bf16[4,128,256]{2,1,0:T(8,128)(2,1)S(1)} %broadcast_in_dim.8), channel_id=1, replica_groups=mesh['y'=4,'zh'=4,'x'=4,'zl'=4,'core'=2] {'zl'}, dimensions={0} | all-to-all | bytes 524288 | tf_op jit(solution)/shard_map/all_to_all | solution.py:16
  27.7 1.1 broadcast_in_dim.9
  28.8 4.0 %all-to-all-start.1 = ((bf16[4,4,128,256]{3,2,1,0:T(8,128)(2,1)}), bf16[4,4,128,256]{3,2,1,0:T(8,128)(2,1)S(1)}, u32[]{:S(2)}, u32[]{:S(2)}) async-start(bf16[4,4,128,256]{3,2,1,0:T(8,128)(2,1)} %broadcast_in_dim.9), calls=%async_computation.1 | async-start | bytes 2097152 | tf_op jit(solution)/shard_map/all_to_all | solution.py:16
  32.8 0.0 copy-done.2
  32.8 3.2 %collective-permute-start.1 = (bf16[512,256]{1,0:T(8,128)(2,1)S(1)}, bf16[512,256]{1,0:T(8,128)(2,1)S(1)}, u32[]{:S(2)}, u32[]{:S(2)}) collective-permute-start(bf16[512,256]{1,0:T(8,128)(2,1)S(1)} %copy-done.2), channel_id=1, source_target_pairs={{0,128},{128,256},{256,384},{384,0},{1,129},{129,257},{257,385},{3... | collective-permute-start | bytes 786440 | tf_op jit(solution)/shard_map/ppermute | solution.py:24
  36.0 4.5 %collective-permute-start.2 = (bf16[512,256]{1,0:T(8,128)(2,1)S(1)}, bf16[512,256]{1,0:T(8,128)(2,1)S(1)}, u32[]{:S(2)}, u32[]{:S(2)}) collective-permute-start(bf16[512,256]{1,0:T(8,128)(2,1)S(1)} %copy-done.2), channel_id=1, source_target_pairs={{0,256},{128,384},{256,0},{384,128},{1,257},{129,385},{257,1},{385... | collective-permute-start | bytes 786440 | tf_op jit(solution)/shard_map/ppermute | solution.py:24
  40.5 3.0 %collective-permute-start.3 = (bf16[512,256]{1,0:T(8,128)(2,1)S(1)}, bf16[512,256]{1,0:T(8,128)(2,1)S(1)}, u32[]{:S(2)}, u32[]{:S(2)}) collective-permute-start(bf16[512,256]{1,0:T(8,128)(2,1)S(1)} %copy-done.2), channel_id=1, source_target_pairs={{0,384},{128,0},{256,128},{384,256},{1,385},{129,1},{257,129},{385... | collective-permute-start | bytes 786440 | tf_op jit(solution)/shard_map/ppermute | solution.py:24
  43.5 0.0 collective-permute-done.1.refs_1_
  43.5 3.1 %collective-permute-done.2.refs_2_ = bf16[512,256]{1,0:T(8,128)(2,1)S(1)} collective-permute-done((bf16[512,256]{1,0:T(8,128)(2,1)S(1)}, bf16[512,256]{1,0:T(8,128)(2,1)S(1)}, u32[]{:S(2)}, u32[]{:S(2)}) %collective-permute-start.2) | collective-permute-done | bytes 262176 | tf_op jit(solution)/shard_map/ppermute | solution.py:24
  46.6 3.4 %collective-permute-done.3.refs_3_ = bf16[512,256]{1,0:T(8,128)(2,1)S(1)} collective-permute-done((bf16[512,256]{1,0:T(8,128)(2,1)S(1)}, bf16[512,256]{1,0:T(8,128)(2,1)S(1)}, u32[]{:S(2)}, u32[]{:S(2)}) %collective-permute-start.3) | collective-permute-done | bytes 262176 | tf_op jit(solution)/shard_map/ppermute | solution.py:24
  50.0 0.0 all-to-all-done.1.refs_4_
  50.0 5.8 %collective-permute-start.4 = (bf16[4,4,128,256]{3,2,1,0:T(8,128)(2,1)S(1)}, bf16[4,4,128,256]{3,2,1,0:T(8,128)(2,1)S(1)}, u32[]{:S(2)}, u32[]{:S(2)}) collective-permute-start(bf16[4,4,128,256]{3,2,1,0:T(8,128)(2,1)S(1)} %all-to-all-done.1.refs_4_), channel_id=1, source_target_pairs={{0,1},{1,0},{2,3},{3,2},{4,5},{5,4},{6,7},{7,6},{8,9},{9,8},{10,11... | collective-permute-start | bytes 3145736 | tf_op jit(solution)/shard_map/ppermute | solution.py:24
  55.9 0.1 pad_add_fusion.where
  55.9 0.1 pad_add_fusion.1.where
  56.0 0.0 copy-start.6
  56.0 1.0 shard_map.64.refs_5_
  57.0 1.1 collective-permute-done.4.refs_4_
  58.1 0.0 copy-start
  58.1 1.1 shard_map.65
  59.3 0.0 copy-done.6
  59.3 2.4 %collective-permute-start.5 = (bf16[256,4096]{1,0:T(8,128)(2,1)S(1)}, bf16[256,4096]{1,0:T(8,128)(2,1)S(1)}, u32[]{:S(2)}, u32[]{:S(2)}) collective-permute-start(bf16[256,4096]{1,0:T(8,128)(2,1)S(1)} %copy-done.6), channel_id=1, source_target_pairs={{0,1},{1,0},{2,3},{3,2},{4,5},{5,4},{6,7},{7,6},{8,9},{9,8},{10,11... | collective-permute-start | bytes 6291464 | tf_op jit(solution)/shard_map/ppermute | solution.py:24
  61.7 25.7 %all_to_all.36 = f16[4,144,256]{2,1,0:T(8,128)(2,1)S(1)} all-to-all(f16[4,144,256]{2,1,0:T(8,128)(2,1)S(1)} %convert_element_type.6), channel_id=1, replica_groups=mesh['y'=4,'zh'=4,'x'=4,'zl'=4,'core'=2] {'zh'}, dimensions={0} | all-to-all | bytes 589824 | tf_op jit(solution)/shard_map/all_to_all | solution.py:16
  87.5 0.0 collective-permute-done.5.their_directions.directions
  87.5 0.1 shard_map.66.own
  87.6 5.2 %collective-permute-start.6 = (bf16[128,256]{1,0:T(8,128)(2,1)S(1)}, bf16[128,256]{1,0:T(8,128)(2,1)S(1)}, u32[]{:S(2)}, u32[]{:S(2)}) collective-permute-start(bf16[128,256]{1,0:T(8,128)(2,1)S(1)} %shard_map.66.own), channel_id=1, source_target_pairs={{0,1},{1,0},{2,3},{3,2},{4,5},{5,4},{6,7},{7,6},{8,9},{9,8},{10,11... | collective-permute-start | bytes 196616 | tf_op jit(solution)/shard_map/ppermute | solution.py:24
  92.8 0.9 collective-permute-done.6.theirs
  93.7 0.0 copy-done
  93.7 1.6 shard_map.67
  95.3 0.0 copy-start.3
  95.3 0.0 copy-start.4
  95.3 0.0 copy-start.5
  95.3 18.4 %all_to_all.37.parts = bf16[4,4,128,256]{3,2,1,0:T(8,128)(2,1)S(1)} all-to-all(bf16[4,4,128,256]{3,2,1,0:T(8,128)(2,1)S(1)} %shard_map.67), channel_id=1, replica_groups=mesh['y'=4,'zh'=4,'x'=4,'zl'=4,'core'=2] {'x'}, dimensions={0} | all-to-all | bytes 2097152 | tf_op jit(solution)/shard_map/all_to_all | solution.py:16
  113.8 0.8 shard_map.68
  114.6 6.5 %all-to-all-start.4 = ((bf16[4,128,256]{2,1,0:T(8,128)(2,1)}), bf16[4,128,256]{2,1,0:T(8,128)(2,1)S(1)}, u32[]{:S(2)}, u32[]{:S(2)}) async-start(bf16[4,128,256]{2,1,0:T(8,128)(2,1)} %shard_map.68), calls=%async_computation.4 | async-start | bytes 524288 | tf_op jit(solution)/shard_map/all_to_all | solution.py:16
  121.1 5.7 %all-to-all-done.4.parts = bf16[4,128,256]{2,1,0:T(8,128)(2,1)S(1)} async-done(((bf16[4,128,256]{2,1,0:T(8,128)(2,1)}), bf16[4,128,256]{2,1,0:T(8,128)(2,1)S(1)}, u32[]{:S(2)}, u32[]{:S(2)}) %all-to-all-start.4) | async-done | bytes 262176 | tf_op jit(solution)/shard_map/all_to_all | solution.py:16
  126.8 0.0 copy-done.3
  126.8 0.0 copy-done.4
  126.8 0.0 copy-done.5
  126.8 0.7 shard_map.69
  127.5 10.6 %all_to_all.38 = bf16[4,256,128]{2,1,0:T(8,128)(2,1)S(1)} all-to-all(bf16[4,256,128]{2,1,0:T(8,128)(2,1)S(1)} %broadcast_in_dim.10), channel_id=1, replica_groups=mesh['y'=4,'zh'=4,'x'=4,'zl'=4,'core'=2] {'zl'}, dimensions={0} | all-to-all | bytes 524288 | tf_op jit(solution)/shard_map/all_to_all | solution.py:16
  138.1 0.2 broadcast_in_dim.11
  138.3 0.0 copy-start.1
  138.4 13.9 %all_to_all.39 = bf16[4,4,256,128]{3,2,1,0:T(8,128)(2,1)S(1)} all-to-all(bf16[4,4,256,128]{3,2,1,0:T(8,128)(2,1)S(1)} %broadcast_in_dim.11), channel_id=1, replica_groups=mesh['y'=4,'zh'=4,'x'=4,'zl'=4,'core'=2] {'x'}, dimensions={0} | all-to-all | bytes 2097152 | tf_op jit(solution)/shard_map/all_to_all | solution.py:16
  152.2 1.4 shard_map.71
  153.6 6.8 %collective-permute-start.7 = (f32[256,128]{1,0:T(8,128)S(1)}, f32[256,128]{1,0:T(8,128)S(1)}, u32[]{:S(2)}, u32[]{:S(2)}) collective-permute-start(f32[256,128]{1,0:T(8,128)S(1)} %shard_map.71), channel_id=1, source_target_pairs={{0,1},{1,0},{2,3},{3,2},{4,5},{5,4},{6,7},{7,6},{8,9},{9,8},{10,11... | collective-permute-start | bytes 393224 | tf_op jit(solution)/shard_map/ppermute | solution.py:24
  160.4 0.0 copy-done.1
  160.4 1.4 shard_map.70
  161.8 0.0 collective-permute-done.7
  161.8 0.7 add.15
  (4 shorter events, 0.1 us)
Async XLA Ops:
  0.0 4.6 %collective-permute-start = (bf16[128,256]{0,1:T(8,128)(2,1)}, bf16[128,256]{0,1:T(8,128)(2,1)S(1)}, u32[]{:S(2)}, u32[]{:S(2)}) collective-permute-start(bf16[128,256]{0,1:T(8,128)(2,1)} %bitcast.12), channel_id=1, source_target_pairs={{0,0},{2,32},{4,64},{6,96},{32,2},{34,34},{36,66},{38,98},{64,4},{... | collective-permute-start | bytes 196616 | tf_op jit(solution)/shard_map/ppermute | solution.py:237
  4.8 28.0 %copy-start.2 = (bf16[512,256]{1,0:T(8,128)(2,1)S(1)}, bf16[512,256]{1,0:T(8,128)(2,1)}, u32[]{:S(2)}) copy-start(bf16[512,256]{1,0:T(8,128)(2,1)} %refs_0_.1) | copy-start | bytes 786436
  28.8 21.3 %all-to-all-start.1 = ((bf16[4,4,128,256]{3,2,1,0:T(8,128)(2,1)}), bf16[4,4,128,256]{3,2,1,0:T(8,128)(2,1)S(1)}, u32[]{:S(2)}, u32[]{:S(2)}) async-start(bf16[4,4,128,256]{3,2,1,0:T(8,128)(2,1)} %broadcast_in_dim.9), calls=%async_computation.1 | async-start | bytes 2097152 | tf_op jit(solution)/shard_map/all_to_all | solution.py:16
  32.8 10.7 %collective-permute-start.1 = (bf16[512,256]{1,0:T(8,128)(2,1)S(1)}, bf16[512,256]{1,0:T(8,128)(2,1)S(1)}, u32[]{:S(2)}, u32[]{:S(2)}) collective-permute-start(bf16[512,256]{1,0:T(8,128)(2,1)S(1)} %copy-done.2), channel_id=1, source_target_pairs={{0,128},{128,256},{256,384},{384,0},{1,129},{129,257},{257,385},{3... | collective-permute-start | bytes 786440 | tf_op jit(solution)/shard_map/ppermute | solution.py:24
  36.0 10.6 %collective-permute-start.2 = (bf16[512,256]{1,0:T(8,128)(2,1)S(1)}, bf16[512,256]{1,0:T(8,128)(2,1)S(1)}, u32[]{:S(2)}, u32[]{:S(2)}) collective-permute-start(bf16[512,256]{1,0:T(8,128)(2,1)S(1)} %copy-done.2), channel_id=1, source_target_pairs={{0,256},{128,384},{256,0},{384,128},{1,257},{129,385},{257,1},{385... | collective-permute-start | bytes 786440 | tf_op jit(solution)/shard_map/ppermute | solution.py:24
  40.5 9.5 %collective-permute-start.3 = (bf16[512,256]{1,0:T(8,128)(2,1)S(1)}, bf16[512,256]{1,0:T(8,128)(2,1)S(1)}, u32[]{:S(2)}, u32[]{:S(2)}) collective-permute-start(bf16[512,256]{1,0:T(8,128)(2,1)S(1)} %copy-done.2), channel_id=1, source_target_pairs={{0,384},{128,0},{256,128},{384,256},{1,385},{129,1},{257,129},{385... | collective-permute-start | bytes 786440 | tf_op jit(solution)/shard_map/ppermute | solution.py:24
  50.0 8.1 %collective-permute-start.4 = (bf16[4,4,128,256]{3,2,1,0:T(8,128)(2,1)S(1)}, bf16[4,4,128,256]{3,2,1,0:T(8,128)(2,1)S(1)}, u32[]{:S(2)}, u32[]{:S(2)}) collective-permute-start(bf16[4,4,128,256]{3,2,1,0:T(8,128)(2,1)S(1)} %all-to-all-done.1.refs_4_), channel_id=1, source_target_pairs={{0,1},{1,0},{2,3},{3,2},{4,5},{5,4},{6,7},{7,6},{8,9},{9,8},{10,11... | collective-permute-start | bytes 3145736 | tf_op jit(solution)/shard_map/ppermute | solution.py:24
  56.0 3.2 %copy-start.6 = (bf16[256,4096]{1,0:T(8,128)(2,1)S(1)}, bf16[256,4096]{1,0:T(8,128)(2,1)}, u32[]{:S(2)}) copy-start(bf16[256,4096]{1,0:T(8,128)(2,1)} %constant_dynamic-slice_fusion) | copy-start | bytes 6291460
  58.1 35.5 %copy-start = (bf16[256,8192]{1,0:T(8,128)(2,1)S(1)}, bf16[256,8192]{1,0:T(8,128)(2,1)}, u32[]{:S(2)}) copy-start(bf16[256,8192]{1,0:T(8,128)(2,1)} %directions.3) | copy-start | bytes 12582916
  59.3 28.2 %collective-permute-start.5 = (bf16[256,4096]{1,0:T(8,128)(2,1)S(1)}, bf16[256,4096]{1,0:T(8,128)(2,1)S(1)}, u32[]{:S(2)}, u32[]{:S(2)}) collective-permute-start(bf16[256,4096]{1,0:T(8,128)(2,1)S(1)} %copy-done.6), channel_id=1, source_target_pairs={{0,1},{1,0},{2,3},{3,2},{4,5},{5,4},{6,7},{7,6},{8,9},{9,8},{10,11... | collective-permute-start | bytes 6291464 | tf_op jit(solution)/shard_map/ppermute | solution.py:24
  87.6 6.1 %collective-permute-start.6 = (bf16[128,256]{1,0:T(8,128)(2,1)S(1)}, bf16[128,256]{1,0:T(8,128)(2,1)S(1)}, u32[]{:S(2)}, u32[]{:S(2)}) collective-permute-start(bf16[128,256]{1,0:T(8,128)(2,1)S(1)} %shard_map.66.own), channel_id=1, source_target_pairs={{0,1},{1,0},{2,3},{3,2},{4,5},{5,4},{6,7},{7,6},{8,9},{9,8},{10,11... | collective-permute-start | bytes 196616 | tf_op jit(solution)/shard_map/ppermute | solution.py:24
  95.3 31.5 %copy-start.3 = (f32[8192]{0:T(1024)S(1)}, f32[8192]{0:T(1024)}, u32[]{:S(2)}) copy-start(f32[8192]{0:T(1024)} %param.9) | copy-start | bytes 98308
  95.3 31.5 %copy-start.4 = (s32[128]{0:T(128)S(1)}, s32[128]{0:T(128)}, u32[]{:S(2)}) copy-start(s32[128]{0:T(128)} %param.11) | copy-start | bytes 1540
  95.3 31.5 %copy-start.5 = (f32[16]{0:T(128)S(1)}, f32[16]{0:T(128)}, u32[]{:S(2)}) copy-start(f32[16]{0:T(128)} %grid_values.1) | copy-start | bytes 196
  114.6 12.2 %all-to-all-start.4 = ((bf16[4,128,256]{2,1,0:T(8,128)(2,1)}), bf16[4,128,256]{2,1,0:T(8,128)(2,1)S(1)}, u32[]{:S(2)}, u32[]{:S(2)}) async-start(bf16[4,128,256]{2,1,0:T(8,128)(2,1)} %shard_map.68), calls=%async_computation.4 | async-start | bytes 524288 | tf_op jit(solution)/shard_map/all_to_all | solution.py:16
  138.3 22.1 %copy-start.1 = (bf16[256,8192]{1,0:T(8,128)(2,1)S(1)}, bf16[256,8192]{1,0:T(8,128)(2,1)}, u32[]{:S(2)}) copy-start(bf16[256,8192]{1,0:T(8,128)(2,1)} %directions.3) | copy-start | bytes 12582916
  153.6 8.2 %collective-permute-start.7 = (f32[256,128]{1,0:T(8,128)S(1)}, f32[256,128]{1,0:T(8,128)S(1)}, u32[]{:S(2)}, u32[]{:S(2)}) collective-permute-start(f32[256,128]{1,0:T(8,128)S(1)} %shard_map.71), channel_id=1, source_target_pairs={{0,1},{1,0},{2,3},{3,2},{4,5},{5,4},{6,7},{7,6},{8,9},{9,8},{10,11... | collective-permute-start | bytes 393224 | tf_op jit(solution)/shard_map/ppermute | solution.py:24

commit v3 on v2

--- a/solution.py
+++ b/solution.py
@@ -28,21 +28,35 @@
     return [pl.BlockSpec(memory_space=pltpu.VMEM)] * count
 
 
-def cross_kernel(ny, block, first, where, *refs):
-    features, signals, total, out = refs[:ny], refs[ny], refs[-2], refs[-1]
-    start = pl.multiple_of(where[1] * block, block)
-    groups, voxels, _ = signals.shape[1:]
-    acc = None if first else total[...]
+def cross_kernel(ny, which, y, signals, *refs):
+    features, out = refs[:ny], refs[ny]
+    groups, voxels, block = signals.shape[1:]
+    acc = None
     for k in range(ny):
-        other = lax.rem(where[0] - k + ny, ny)
-        left = signals[other].reshape(groups * voxels, block)
-        right = features[k][pl.ds(start, block), :]
-        term = jnp.dot(left, right, preferred_element_type=F32)
+        left = signals[lax.rem(y[0] - k + ny, ny)].reshape(groups * voxels, block)
+        term = jnp.dot(left, features[k][which], preferred_element_type=F32)
         acc = term if acc is None else acc + term
-    if first:
-        out[...] = acc
-        return
-    acc = acc * (1.0 / (ny * groups * 2 * block))
+    out[...] = acc
+
+
+def cross_products(which, y, signals, features):
+    ny, (_, block, rows) = len(features), features[0].shape
+    _, groups, voxels, _ = signals.shape
+    return pl.pallas_call(
+        functools.partial(cross_kernel, ny, which),
+        out_shape=jax.ShapeDtypeStruct((groups * voxels, rows), F32),
+        in_specs=[pl.BlockSpec(memory_space=pltpu.SMEM)] + whole(1 + ny),
+        out_specs=pl.BlockSpec(memory_space=pltpu.VMEM),
+        compiler_params=pltpu.CompilerParams(vmem_limit_bytes=16 << 20),
+        cost_estimate=pl.CostEstimate(
+            flops=2 * ny * block * groups * voxels * rows, bytes_accessed=4 << 20, transcendentals=0
+        ),
+    )(y, signals, *features)
+
+
+def scale_kernel(total_time, kept, received, out):
+    groups, voxels = out.shape[0], out.shape[1] - EXTRA
+    acc = (kept[...] + received[...]) * (1.0 / total_time)
     top = jnp.max(jnp.max(jnp.abs(acc), axis=0, keepdims=True), axis=1, keepdims=True)
     scale, exponent = jnp.ones_like(top), jnp.zeros_like(top)
     for step in STEPS:
@@ -54,22 +68,18 @@
     out[:, voxels:, :] = jnp.broadcast_to(exponent[None], (groups, EXTRA, acc.shape[1]))
 
 
-def cross_products(where, features, signals, total):
-    ny, (time, rows) = len(features), features[0].shape
-    _, groups, voxels, block = signals.shape
-    first = total is None
-    operands = list(features) + [signals] + ([] if first else [total])
-    shape = (groups * voxels, rows) if first else (groups, voxels + EXTRA, rows)
-    return pl.pallas_call(
-        functools.partial(cross_kernel, ny, block, first),
-        out_shape=jax.ShapeDtypeStruct(shape, F32),
-        in_specs=[pl.BlockSpec(memory_space=pltpu.SMEM)] + whole(len(operands)),
-        out_specs=pl.BlockSpec(memory_space=pltpu.VMEM),
-        compiler_params=pltpu.CompilerParams(vmem_limit_bytes=16 << 20),
-        cost_estimate=pl.CostEstimate(
-            flops=2 * ny * block * groups * voxels * rows, bytes_accessed=4 << 20, transcendentals=0
-        ),
-    )(where, *operands)
+def scaled(kept, received, groups, total_time):
+    rows, width = kept.shape
+    return pl.pallas_call(
+        functools.partial(scale_kernel, total_time),
+        out_shape=jax.ShapeDtypeStruct((groups, rows // groups + EXTRA, width), F32),
+        in_specs=whole(2),
+        out_specs=pl.BlockSpec(memory_space=pltpu.VMEM),
+        compiler_params=pltpu.CompilerParams(vmem_limit_bytes=16 << 20),
+        cost_estimate=pl.CostEstimate(
+            flops=5 * kept.size, bytes_accessed=12 * kept.size, transcendentals=0
+        ),
+    )(kept, received)
 
 
 def covariance_kernel(parts, out):
@@ -101,19 +111,19 @@
     )(parts)
 
 
-def rotate_kernel(half, own, directions, theirs, their_directions, out):
-    product = jnp.dot(own[...], directions[...], preferred_element_type=F32)
-    product += jnp.dot(theirs[...], their_directions[...], preferred_element_type=F32)
+def rotate_kernel(half, covariances, directions, their_directions, out):
+    own, theirs = covariances[half[0]], covariances[1 - half[0]]
+    product = jnp.dot(own, directions[...], preferred_element_type=F32)
+    product += jnp.dot(theirs, their_directions[...], preferred_element_type=F32)
     share = out.shape[-1]
     for j in range(out.shape[1]):
         out[0, j] = product[:, j * share : (j + 1) * share].astype(out.dtype)
 
 
-def rotate(half, own, directions, theirs, their_directions, nx, nzl):
-    voxels, rows = own.shape
+def rotate(half, covariances, directions, their_directions, nx, nzl):
+    _, voxels, rows = covariances.shape
     columns = their_directions.shape[1] // nx
     share = columns // nzl
-    flat = pl.BlockSpec((voxels, rows), lambda i, h: (0, 0))
     return pl.pallas_call(
         rotate_kernel,
         out_shape=jax.ShapeDtypeStruct((nx, nzl, voxels, share), BF16),
@@ -121,9 +131,8 @@
             num_scalar_prefetch=1,
             grid=(nx,),
             in_specs=[
-                flat,
+                pl.BlockSpec(covariances.shape, lambda i, h: (0, 0, 0)),
                 pl.BlockSpec((rows, columns), lambda i, h: (0, h[0] * nx + i)),
-                flat,
                 pl.BlockSpec((rows, columns), lambda i, h: (0, i)),
             ],
             out_specs=pl.BlockSpec((1, nzl, voxels, share), lambda i, h: (i, 0, 0, 0)),
@@ -132,7 +141,7 @@
         cost_estimate=pl.CostEstimate(
             flops=4 * rows * columns * nx * voxels, bytes_accessed=4 << 20, transcendentals=0
         ),
-    )(half, own, directions, theirs, their_directions)
+    )(half, covariances, directions, their_directions)
 
 
 def add_kernel(parts, out):
@@ -230,30 +239,32 @@
     ny, nzh, nx, nzl = (lax.axis_size(a) for a in ("y", "zh", "x", "zl"))
     width = spectral_directions.shape[1]
     core = lax.axis_index("core")
-    mine, other = core.reshape(1), (1 - core).reshape(1)
+    mine = core.reshape(1)
     y = lax.axis_index("y").reshape(1)
 
     swap = [(a * nzl + b, b * nzl + a) for a in range(nzh) for b in range(nzl)]
     signals = lax.ppermute(measured_signals.T, ("zh", "zl"), swap)
     given = lax.dynamic_slice_in_dim(spectral_directions, (1 - core) * (width // 2), width // 2, axis=1)
-    features = [hidden_states] + [shift(hidden_states, "y", ny, k) for k in range(1, ny)]
-    signals, given = lax.optimization_barrier((signals, given))
+    half = hidden_states.shape[0] // 2
+    kept = lax.dynamic_slice_in_dim(hidden_states, core * half, half)
+    swapped = shift(lax.dynamic_slice_in_dim(hidden_states, (1 - core) * half, half), "core", 2, 1)
+    features = jnp.stack([kept, swapped])
+    signals, given, features = lax.optimization_barrier((signals, given, features))
     signals = gather(signals, "zl", nzl)
+    features = [features] + [shift(features, "y", ny, k) for k in range(1, ny)]
     signals = gather(signals, "x", nx)
     signals, *features = lax.optimization_barrier((signals, *features))
-    signals_other = shift(signals, "core", 2, 1)
-    cross = cross_products(jnp.concatenate([y, mine]), features, signals, None)
-    cross = cross_products(jnp.concatenate([y, other]), features, signals_other, cross)
+    received = shift(cross_products(1, y, signals, features), "core", 2, 1)
+    kept = cross_products(0, y, signals, features)
+    cross = scaled(kept, received, nzh, 2 * half * ny * nzh)
+
     cross, given = lax.optimization_barrier((cross, given))
     their_directions = shift(given, "core", 2, 1)
     parts = exchange(cross.astype(F16), "zh").astype(F32)
-    parts, their_directions = lax.optimization_barrier((parts, their_directions))
 
     covariance = rounded_covariance(parts)
-    their_covariance = shift(covariance, "core", 2, 1)
-    rotated = rotate(
-        mine, covariance, spectral_directions, their_covariance, their_directions, nx, nzl
-    )
+    covariances = lax.all_gather(covariance, "core", axis=0, tiled=False)
+    rotated = rotate(mine, covariances, spectral_directions, their_directions, nx, nzl)
     rotated = exchange(rotated, "x")
     rotated = exchange(add_parts(rotated), "zl")
     index = (core * nx + lax.axis_index("x")) * nzl + lax.axis_index("zl")

time: 163 us -> 161 us (0.988)
  blocking collectives: 91.5 us -> 87.5 us
    all_to_all x5, blocking collectives: 91.5 us -> 82.7 us  [exchange(): return lax.all_to_all(blocks, axis, 0, 0, tiled=True)]
    all_gather x0 -> x1, blocking collectives: none -> 4.84 us  [per_device(): covariances = lax.all_gather(covariance, 'core', axis=0, tiled=False)]
    ppermute x7, starting transfers between devices: 30.9 us -> 32.5 us  [shift(): lax.ppermute(block, axis, [(i, (i + by) % size) for i in range(size)])]
  transfers between devices with their start and end apart: 10 -> 10, of which waited for: 5 -> 4; matrix products, arithmetic and copies ran while one was open for 2% -> 3% of each run, Pallas kernels for 1% -> 1%
where the time goes in v3:
time: 161 us; the launch traced here: 160 us
  blocking collectives  87.5 us (54%)
  starting transfers between devices  44.5 us (28%)
  waiting for transfers between devices  14 us (9%)
  Pallas kernels  7.1 us (4%)
  local copies, waits for them, and re-layouts  5.61 us (3%)
    all_to_all x5, blocking collectives, exchange(): return lax.all_to_all(blocks, axis, 0, 0, tiled=True)  82.7 us
    ppermute x7, starting transfers between devices, shift(): lax.ppermute(block, axis, [(i, (i + by) % size) for i in range(size)])  32.5 us
    all_to_all x2, starting transfers between devices, exchange(): return lax.all_to_all(blocks, axis, 0, 0, tiled=True)  10.5 us
    ppermute x7, waiting for transfers between devices, shift(): lax.ppermute(block, axis, [(i, (i + by) % size) for i in range(size)])  8.35 us
    all_to_all x2, waiting for transfers between devices, exchange(): return lax.all_to_all(blocks, axis, 0, 0, tiled=True)  5.68 us
    all_gather x1, blocking collectives, per_device(): covariances = lax.all_gather(covariance, 'core', axis=0, tiled=False)  4.84 us
  transfers between devices with their start and end apart: 10, of which 4 were waited for; matrix products, arithmetic and copies ran while one was open for 3% of the time, Pallas kernels for 1%

profile of v3, /device:TPU:1, one launch (start us, length us, event | category | flops | bytes accessed | tf_op | source)
XLA Modules:
  0.0 159.9 jit_solution(1362463028317042047)
XLA Ops:
  0.0 1.5 collective-permute-start
  1.5 1.0 dynamic-slice_bitcast_fusion
  2.5 8.8 %collective-permute-start.1 = (bf16[256,256]{1,0:T(8,128)(2,1)S(1)}, bf16[256,256]{1,0:T(8,128)(2,1)S(1)}, u32[]{:S(2)}, u32[]{:S(2)}) collective-permute-start(bf16[256,256]{1,0:T(8,128)(2,1)S(1)} %get-tuple-element.26), channel_id=1, source_target_pairs={{0,1},{1,0},{2,3},{3,2},{4,5},{5,4},{6,7},{7,6},{8,9},{9,8},{10,11... | collective-permute-start | bytes 393224 | tf_op jit(solution)/shard_map/ppermute | solution.py:24
  11.3 3.2 %constant_dynamic-slice_fusion.1 = bf16[256,4096]{1,0:T(8,128)(2,1)} fusion(bf16[256,8192]{1,0:T(8,128)(2,1)} %directions.3, s32[]{:T(128)S(6)} %select_n.9), kind=kLoop, calls=%fused_computation.3 | loop fusion | bytes 4194308 | tf_op jit(solution)/shard_map/dynamic_slice | solution.py:247
  14.4 0.0 collective-permute-done.1
  14.5 0.0 collective-permute-done
  14.5 0.1 copy.7
  14.6 18.6 %all_to_all.35 = bf16[4,128,256]{2,1,0:T(8,128)(2,1)S(1)} all-to-all(bf16[4,128,256]{2,1,0:T(8,128)(2,1)S(1)} %broadcast_in_dim.8), channel_id=1, replica_groups=mesh['y'=4,'zh'=4,'x'=4,'zl'=4,'core'=2] {'zl'}, dimensions={0} | all-to-all | bytes 524288 | tf_op jit(solution)/shard_map/all_to_all | solution.py:16
  33.2 1.1 broadcast_in_dim.9
  34.3 4.0 %all-to-all-start.1 = ((bf16[4,4,128,256]{3,2,1,0:T(8,128)(2,1)}), bf16[4,4,128,256]{3,2,1,0:T(8,128)(2,1)S(1)}, u32[]{:S(2)}, u32[]{:S(2)}) async-start(bf16[4,4,128,256]{3,2,1,0:T(8,128)(2,1)} %broadcast_in_dim.9), calls=%async_computation.1 | async-start | bytes 2097152 | tf_op jit(solution)/shard_map/all_to_all | solution.py:16
  38.3 3.2 %collective-permute-start.2 = (bf16[2,256,256]{2,1,0:T(8,128)(2,1)S(1)}, bf16[2,256,256]{2,1,0:T(8,128)(2,1)S(1)}, u32[]{:S(2)}, u32[]{:S(2)}) collective-permute-start(bf16[2,256,256]{2,1,0:T(8,128)(2,1)S(1)} %pad_maximum_fusion.refs_0_), channel_id=1, source_target_pairs={{0,128},{128,256},{256,384},{384,0},{1,129},{129,257},{257,385},{3... | collective-permute-start | bytes 786440 | tf_op jit(solution)/shard_map/ppermute | solution.py:24
  41.5 4.5 %collective-permute-start.3 = (bf16[2,256,256]{2,1,0:T(8,128)(2,1)S(1)}, bf16[2,256,256]{2,1,0:T(8,128)(2,1)S(1)}, u32[]{:S(2)}, u32[]{:S(2)}) collective-permute-start(bf16[2,256,256]{2,1,0:T(8,128)(2,1)S(1)} %pad_maximum_fusion.refs_0_), channel_id=1, source_target_pairs={{0,256},{128,384},{256,0},{384,128},{1,257},{129,385},{257,1},{385... | collective-permute-start | bytes 786440 | tf_op jit(solution)/shard_map/ppermute | solution.py:24
  46.0 3.0 %collective-permute-start.4 = (bf16[2,256,256]{2,1,0:T(8,128)(2,1)S(1)}, bf16[2,256,256]{2,1,0:T(8,128)(2,1)S(1)}, u32[]{:S(2)}, u32[]{:S(2)}) collective-permute-start(bf16[2,256,256]{2,1,0:T(8,128)(2,1)S(1)} %pad_maximum_fusion.refs_0_), channel_id=1, source_target_pairs={{0,384},{128,0},{256,128},{384,256},{1,385},{129,1},{257,129},{385... | collective-permute-start | bytes 786440 | tf_op jit(solution)/shard_map/ppermute | solution.py:24
  49.0 0.0 collective-permute-done.2.refs_1_
  49.0 5.3 %collective-permute-done.3.refs_2_ = bf16[2,256,256]{2,1,0:T(8,128)(2,1)S(1)} collective-permute-done((bf16[2,256,256]{2,1,0:T(8,128)(2,1)S(1)}, bf16[2,256,256]{2,1,0:T(8,128)(2,1)S(1)}, u32[]{:S(2)}, u32[]{:S(2)}) %collective-permute-start.3) | collective-permute-done | bytes 262176 | tf_op jit(solution)/shard_map/ppermute | solution.py:24
  54.3 2.0 %collective-permute-done.4.refs_3_ = bf16[2,256,256]{2,1,0:T(8,128)(2,1)S(1)} collective-permute-done((bf16[2,256,256]{2,1,0:T(8,128)(2,1)S(1)}, bf16[2,256,256]{2,1,0:T(8,128)(2,1)S(1)}, u32[]{:S(2)}, u32[]{:S(2)}) %collective-permute-start.4) | collective-permute-done | bytes 262176 | tf_op jit(solution)/shard_map/ppermute | solution.py:24
  56.3 0.0 all-to-all-done.1.signals
  56.3 0.4 shard_map.65
  56.8 0.0 copy-start.5
  56.8 4.0 %collective-permute-start.5 = (f32[512,256]{1,0:T(8,128)S(1)}, f32[512,256]{1,0:T(8,128)S(1)}, u32[]{:S(2)}, u32[]{:S(2)}) collective-permute-start(f32[512,256]{1,0:T(8,128)S(1)} %shard_map.65), channel_id=1, source_target_pairs={{0,1},{1,0},{2,3},{3,2},{4,5},{5,4},{6,7},{7,6},{8,9},{9,8},{10,11... | collective-permute-start | bytes 1572872 | tf_op jit(solution)/shard_map/ppermute | solution.py:24
  60.8 0.4 shard_map.64.kept
  61.2 0.0 copy-start
  61.3 1.1 collective-permute-done.5.received
  62.3 0.2 shard_map.66
  62.5 0.0 copy-done.5
  62.5 2.3 %collective-permute-start.6 = (bf16[256,4096]{1,0:T(8,128)(2,1)S(1)}, bf16[256,4096]{1,0:T(8,128)(2,1)S(1)}, u32[]{:S(2)}, u32[]{:S(2)}) collective-permute-start(bf16[256,4096]{1,0:T(8,128)(2,1)S(1)} %copy-done.5), channel_id=1, source_target_pairs={{0,1},{1,0},{2,3},{3,2},{4,5},{5,4},{6,7},{7,6},{8,9},{9,8},{10,11... | collective-permute-start | bytes 6291464 | tf_op jit(solution)/shard_map/ppermute | solution.py:24
  64.9 21.2 %all_to_all.36 = f16[4,144,256]{2,1,0:T(8,128)(2,1)S(1)} all-to-all(f16[4,144,256]{2,1,0:T(8,128)(2,1)S(1)} %convert_element_type.6), channel_id=1, replica_groups=mesh['y'=4,'zh'=4,'x'=4,'zl'=4,'core'=2] {'zh'}, dimensions={0} | all-to-all | bytes 589824 | tf_op jit(solution)/shard_map/all_to_all | solution.py:16
  86.1 0.1 shard_map.67
  86.2 4.8 %all-gather = bf16[256,256]{1,0:T(8,128)(2,1)S(1)} all-gather(bf16[128,256]{1,0:T(8,128)(2,1)S(1)} %shard_map.67), channel_id=2, replica_groups=mesh['y'=4,'zh'=4,'x'=4,'zl'=4,'core'=2] {'core'}, dimensions={0}, use_global_device_ids=true | all-gather | bytes 196608 | tf_op jit(solution)/shard_map/all_gather | solution.py:266
  91.0 0.0 collective-permute-done.6.their_directions.directions
  91.0 0.0 copy-done
  91.0 1.6 %shard_map.68 = bf16[4,4,128,256]{3,2,1,0:T(8,128)(2,1)S(1)} custom-call(s32[1]{0:T(128)} %bitcast.half, bf16[2,128,256]{2,1,0:T(8,128)(2,1)S(1)} %bitcast.13, bf16[256,8192]{1,0:T(8,128)(2,1)S(1)} %copy-done, bf16[256,4096]{1,0:T(8,128)(2,1)S(1)} %collective-permute-done.6.their_directions.directions), custom_call_target="tpu_custom_call" | custom-call | flops 536870912 | bytes 4194304 | tf_op jit(solution)/shard_map/pallas_call | solution.py:127
  92.7 0.0 copy-start.2
  92.7 0.0 copy-start.3
  92.7 0.0 copy-start.4
  92.7 18.4 %all_to_all.37.parts = bf16[4,4,128,256]{3,2,1,0:T(8,128)(2,1)S(1)} all-to-all(bf16[4,4,128,256]{3,2,1,0:T(8,128)(2,1)S(1)} %shard_map.68), channel_id=1, replica_groups=mesh['y'=4,'zh'=4,'x'=4,'zl'=4,'core'=2] {'x'}, dimensions={0} | all-to-all | bytes 2097152 | tf_op jit(solution)/shard_map/all_to_all | solution.py:16
  111.1 0.8 shard_map.69
  112.0 6.5 %all-to-all-start.4 = ((bf16[4,128,256]{2,1,0:T(8,128)(2,1)}), bf16[4,128,256]{2,1,0:T(8,128)(2,1)S(1)}, u32[]{:S(2)}, u32[]{:S(2)}) async-start(bf16[4,128,256]{2,1,0:T(8,128)(2,1)} %shard_map.69), calls=%async_computation.4 | async-start | bytes 524288 | tf_op jit(solution)/shard_map/all_to_all | solution.py:16
  118.4 5.7 %all-to-all-done.4.parts = bf16[4,128,256]{2,1,0:T(8,128)(2,1)S(1)} async-done(((bf16[4,128,256]{2,1,0:T(8,128)(2,1)}), bf16[4,128,256]{2,1,0:T(8,128)(2,1)S(1)}, u32[]{:S(2)}, u32[]{:S(2)}) %all-to-all-start.4) | async-done | bytes 262176 | tf_op jit(solution)/shard_map/all_to_all | solution.py:16
  124.1 0.0 copy-done.2
  124.1 0.0 copy-done.3
  124.1 0.0 copy-done.4
  124.1 0.7 shard_map.70
  124.9 10.6 %all_to_all.38 = bf16[4,256,128]{2,1,0:T(8,128)(2,1)S(1)} all-to-all(bf16[4,256,128]{2,1,0:T(8,128)(2,1)S(1)} %broadcast_in_dim.10), channel_id=1, replica_groups=mesh['y'=4,'zh'=4,'x'=4,'zl'=4,'core'=2] {'zl'}, dimensions={0} | all-to-all | bytes 524288 | tf_op jit(solution)/shard_map/all_to_all | solution.py:16
  135.5 0.2 broadcast_in_dim.11
  135.7 0.0 copy-start.1
  135.7 13.9 %all_to_all.39 = bf16[4,4,256,128]{3,2,1,0:T(8,128)(2,1)S(1)} all-to-all(bf16[4,4,256,128]{3,2,1,0:T(8,128)(2,1)S(1)} %broadcast_in_dim.11), channel_id=1, replica_groups=mesh['y'=4,'zh'=4,'x'=4,'zl'=4,'core'=2] {'x'}, dimensions={0} | all-to-all | bytes 2097152 | tf_op jit(solution)/shard_map/all_to_all | solution.py:16
  149.6 1.4 shard_map.72
  151.0 6.8 %collective-permute-start.7 = (f32[256,128]{1,0:T(8,128)S(1)}, f32[256,128]{1,0:T(8,128)S(1)}, u32[]{:S(2)}, u32[]{:S(2)}) collective-permute-start(f32[256,128]{1,0:T(8,128)S(1)} %shard_map.72), channel_id=1, source_target_pairs={{0,1},{1,0},{2,3},{3,2},{4,5},{5,4},{6,7},{7,6},{8,9},{9,8},{10,11... | collective-permute-start | bytes 393224 | tf_op jit(solution)/shard_map/ppermute | solution.py:24
  157.8 0.0 copy-done.1
  157.8 1.4 shard_map.71
  159.2 0.0 collective-permute-done.7
  159.2 0.7 add.23
  (5 shorter events, 0.2 us)
Async XLA Ops:
  0.0 14.5 %collective-permute-start = (bf16[128,256]{0,1:T(8,128)(2,1)}, bf16[128,256]{0,1:T(8,128)(2,1)S(1)}, u32[]{:S(2)}, u32[]{:S(2)}) collective-permute-start(bf16[128,256]{0,1:T(8,128)(2,1)} %bitcast.17), channel_id=1, source_target_pairs={{0,0},{2,32},{4,64},{6,96},{32,2},{34,34},{36,66},{38,98},{64,4},{... | collective-permute-start | bytes 196616 | tf_op jit(solution)/shard_map/ppermute | solution.py:246
  2.5 12.0 %collective-permute-start.1 = (bf16[256,256]{1,0:T(8,128)(2,1)S(1)}, bf16[256,256]{1,0:T(8,128)(2,1)S(1)}, u32[]{:S(2)}, u32[]{:S(2)}) collective-permute-start(bf16[256,256]{1,0:T(8,128)(2,1)S(1)} %get-tuple-element.26), channel_id=1, source_target_pairs={{0,1},{1,0},{2,3},{3,2},{4,5},{5,4},{6,7},{7,6},{8,9},{9,8},{10,11... | collective-permute-start | bytes 393224 | tf_op jit(solution)/shard_map/ppermute | solution.py:24
  34.3 22.0 %all-to-all-start.1 = ((bf16[4,4,128,256]{3,2,1,0:T(8,128)(2,1)}), bf16[4,4,128,256]{3,2,1,0:T(8,128)(2,1)S(1)}, u32[]{:S(2)}, u32[]{:S(2)}) async-start(bf16[4,4,128,256]{3,2,1,0:T(8,128)(2,1)} %broadcast_in_dim.9), calls=%async_computation.1 | async-start | bytes 2097152 | tf_op jit(solution)/shard_map/all_to_all | solution.py:16
  38.3 10.7 %collective-permute-start.2 = (bf16[2,256,256]{2,1,0:T(8,128)(2,1)S(1)}, bf16[2,256,256]{2,1,0:T(8,128)(2,1)S(1)}, u32[]{:S(2)}, u32[]{:S(2)}) collective-permute-start(bf16[2,256,256]{2,1,0:T(8,128)(2,1)S(1)} %pad_maximum_fusion.refs_0_), channel_id=1, source_target_pairs={{0,128},{128,256},{256,384},{384,0},{1,129},{129,257},{257,385},{3... | collective-permute-start | bytes 786440 | tf_op jit(solution)/shard_map/ppermute | solution.py:24
  41.5 12.8 %collective-permute-start.3 = (bf16[2,256,256]{2,1,0:T(8,128)(2,1)S(1)}, bf16[2,256,256]{2,1,0:T(8,128)(2,1)S(1)}, u32[]{:S(2)}, u32[]{:S(2)}) collective-permute-start(bf16[2,256,256]{2,1,0:T(8,128)(2,1)S(1)} %pad_maximum_fusion.refs_0_), channel_id=1, source_target_pairs={{0,256},{128,384},{256,0},{384,128},{1,257},{129,385},{257,1},{385... | collective-permute-start | bytes 786440 | tf_op jit(solution)/shard_map/ppermute | solution.py:24
  46.0 10.3 %collective-permute-start.4 = (bf16[2,256,256]{2,1,0:T(8,128)(2,1)S(1)}, bf16[2,256,256]{2,1,0:T(8,128)(2,1)S(1)}, u32[]{:S(2)}, u32[]{:S(2)}) collective-permute-start(bf16[2,256,256]{2,1,0:T(8,128)(2,1)S(1)} %pad_maximum_fusion.refs_0_), channel_id=1, source_target_pairs={{0,384},{128,0},{256,128},{384,256},{1,385},{129,1},{257,129},{385... | collective-permute-start | bytes 786440 | tf_op jit(solution)/shard_map/ppermute | solution.py:24
  56.8 5.8 %copy-start.5 = (bf16[256,4096]{1,0:T(8,128)(2,1)S(1)}, bf16[256,4096]{1,0:T(8,128)(2,1)}, u32[]{:S(2)}) copy-start(bf16[256,4096]{1,0:T(8,128)(2,1)} %constant_dynamic-slice_fusion.1) | copy-start | bytes 6291460
  56.8 5.5 %collective-permute-start.5 = (f32[512,256]{1,0:T(8,128)S(1)}, f32[512,256]{1,0:T(8,128)S(1)}, u32[]{:S(2)}, u32[]{:S(2)}) collective-permute-start(f32[512,256]{1,0:T(8,128)S(1)} %shard_map.65), channel_id=1, source_target_pairs={{0,1},{1,0},{2,3},{3,2},{4,5},{5,4},{6,7},{7,6},{8,9},{9,8},{10,11... | collective-permute-start | bytes 1572872 | tf_op jit(solution)/shard_map/ppermute | solution.py:24
  61.2 29.8 %copy-start = (bf16[256,8192]{1,0:T(8,128)(2,1)S(1)}, bf16[256,8192]{1,0:T(8,128)(2,1)}, u32[]{:S(2)}) copy-start(bf16[256,8192]{1,0:T(8,128)(2,1)} %directions.3) | copy-start | bytes 12582916
  62.5 28.5 %collective-permute-start.6 = (bf16[256,4096]{1,0:T(8,128)(2,1)S(1)}, bf16[256,4096]{1,0:T(8,128)(2,1)S(1)}, u32[]{:S(2)}, u32[]{:S(2)}) collective-permute-start(bf16[256,4096]{1,0:T(8,128)(2,1)S(1)} %copy-done.5), channel_id=1, source_target_pairs={{0,1},{1,0},{2,3},{3,2},{4,5},{5,4},{6,7},{7,6},{8,9},{9,8},{10,11... | collective-permute-start | bytes 6291464 | tf_op jit(solution)/shard_map/ppermute | solution.py:24
  92.7 31.5 %copy-start.2 = (f32[8192]{0:T(1024)S(1)}, f32[8192]{0:T(1024)}, u32[]{:S(2)}) copy-start(f32[8192]{0:T(1024)} %param.9) | copy-start | bytes 98308
  92.7 31.4 %copy-start.3 = (s32[128]{0:T(128)S(1)}, s32[128]{0:T(128)}, u32[]{:S(2)}) copy-start(s32[128]{0:T(128)} %param.11) | copy-start | bytes 1540
  92.7 31.4 %copy-start.4 = (f32[16]{0:T(128)S(1)}, f32[16]{0:T(128)}, u32[]{:S(2)}) copy-start(f32[16]{0:T(128)} %grid_values.1) | copy-start | bytes 196
  112.0 12.2 %all-to-all-start.4 = ((bf16[4,128,256]{2,1,0:T(8,128)(2,1)}), bf16[4,128,256]{2,1,0:T(8,128)(2,1)S(1)}, u32[]{:S(2)}, u32[]{:S(2)}) async-start(bf16[4,128,256]{2,1,0:T(8,128)(2,1)} %shard_map.69), calls=%async_computation.4 | async-start | bytes 524288 | tf_op jit(solution)/shard_map/all_to_all | solution.py:16
  135.7 22.1 %copy-start.1 = (bf16[256,8192]{1,0:T(8,128)(2,1)S(1)}, bf16[256,8192]{1,0:T(8,128)(2,1)}, u32[]{:S(2)}) copy-start(bf16[256,8192]{1,0:T(8,128)(2,1)} %directions.3) | copy-start | bytes 12582916
  151.0 8.2 %collective-permute-start.7 = (f32[256,128]{1,0:T(8,128)S(1)}, f32[256,128]{1,0:T(8,128)S(1)}, u32[]{:S(2)}, u32[]{:S(2)}) collective-permute-start(f32[256,128]{1,0:T(8,128)S(1)} %shard_map.72), channel_id=1, source_target_pairs={{0,1},{1,0},{2,3},{3,2},{4,5},{5,4},{6,7},{7,6},{8,9},{9,8},{10,11... | collective-permute-start | bytes 393224 | tf_op jit(solution)/shard_map/ppermute | solution.py:24

commit v4 on v3

--- a/solution.py
+++ b/solution.py
@@ -8,8 +8,8 @@
 from jax.sharding import Mesh, PartitionSpec as P
 
 F32, BF16, F16 = jnp.float32, jnp.bfloat16, jnp.float16
-STEPS = (64, 32, 16, 8, 4, 2, 1)
-EXTRA = 16
+STEPS = (64, 32, 16, 8, 4, 2)
+EXTRA = 8
 
 
 def exchange(blocks, axis):
@@ -250,9 +250,9 @@
     swapped = shift(lax.dynamic_slice_in_dim(hidden_states, (1 - core) * half, half), "core", 2, 1)
     features = jnp.stack([kept, swapped])
     signals, given, features = lax.optimization_barrier((signals, given, features))
-    signals = gather(signals, "zl", nzl)
     features = [features] + [shift(features, "y", ny, k) for k in range(1, ny)]
-    signals = gather(signals, "x", nx)
+    signals = gather(signals, ("x", "zl"), nx * nzl)
+    signals = signals.reshape((nx, nzl) + signals.shape[1:])
     signals, *features = lax.optimization_barrier((signals, *features))
     received = shift(cross_products(1, y, signals, features), "core", 2, 1)
     kept = cross_products(0, y, signals, features)

time: 161 us -> 156 us (0.969)
  blocking collectives: 87.5 us -> 67.2 us
  waiting for transfers between devices: 14 us -> 23.3 us
  starting transfers between devices: 44.5 us -> 50.6 us
    all_to_all x5 -> x4, blocking collectives: 82.7 us -> 64.5 us  [exchange(): return lax.all_to_all(blocks, axis, 0, 0, tiled=True)]
    all_to_all x2, waiting for transfers between devices: 5.68 us -> 14.4 us  [exchange(): return lax.all_to_all(blocks, axis, 0, 0, tiled=True)]
    all_to_all x2, starting transfers between devices: 10.5 us -> 17.1 us  [exchange(): return lax.all_to_all(blocks, axis, 0, 0, tiled=True)]
    all_gather x1, blocking collectives: 4.84 us -> 2.75 us  [per_device(): covariances = lax.all_gather(covariance, 'core', axis=0, tiled=False)]
  transfers between devices with their start and end apart: 10 -> 10, of which waited for: 4 -> 6; matrix products, arithmetic and copies ran while one was open for 3% -> 3% of each run, Pallas kernels for 1% -> 1%
where the time goes in v4:
time: 156 us; the launch traced here: 155 us
  blocking collectives  67.2 us (43%)
  starting transfers between devices  50.6 us (32%)
  waiting for transfers between devices  23.3 us (15%)
  Pallas kernels  7.1 us (5%)
  local copies, waits for them, and re-layouts  5.59 us (4%)
    all_to_all x4, blocking collectives, exchange(): return lax.all_to_all(blocks, axis, 0, 0, tiled=True)  64.5 us
    ppermute x7, starting transfers between devices, shift(): lax.ppermute(block, axis, [(i, (i + by) % size) for i in range(size)])  32 us
    all_to_all x2, starting transfers between devices, exchange(): return lax.all_to_all(blocks, axis, 0, 0, tiled=True)  17.1 us
    all_to_all x2, waiting for transfers between devices, exchange(): return lax.all_to_all(blocks, axis, 0, 0, tiled=True)  14.4 us
    ppermute x7, waiting for transfers between devices, shift(): lax.ppermute(block, axis, [(i, (i + by) % size) for i in range(size)])  8.98 us
    dynamic_slice x1, local copies, waits for them, and re-layouts, per_device(): lax.dynamic_slice_in_dim(spectral_directions, (1 - core) * (width // 2),...  3.15 us
  transfers between devices with their start and end apart: 10, of which 6 were waited for; matrix products, arithmetic and copies ran while one was open for 3% of the time, Pallas kernels for 1%

profile of v4, /device:TPU:1, one launch (start us, length us, event | category | flops | bytes accessed | tf_op | source)
XLA Modules:
  0.0 154.9 jit_solution(1715324527301755917)
XLA Ops:
  0.0 1.5 collective-permute-start
  1.5 1.0 dynamic-slice_bitcast_fusion
  2.5 8.8 %collective-permute-start.1 = (bf16[256,256]{1,0:T(8,128)(2,1)S(1)}, bf16[256,256]{1,0:T(8,128)(2,1)S(1)}, u32[]{:S(2)}, u32[]{:S(2)}) collective-permute-start(bf16[256,256]{1,0:T(8,128)(2,1)S(1)} %get-tuple-element.26), channel_id=1, source_target_pairs={{0,1},{1,0},{2,3},{3,2},{4,5},{5,4},{6,7},{7,6},{8,9},{9,8},{10,11... | collective-permute-start | bytes 393224 | tf_op jit(solution)/shard_map/ppermute | solution.py:24
  11.3 3.2 %constant_dynamic-slice_fusion.1 = bf16[256,4096]{1,0:T(8,128)(2,1)} fusion(bf16[256,8192]{1,0:T(8,128)(2,1)} %directions.3, s32[]{:T(128)S(6)} %select_n.9), kind=kLoop, calls=%fused_computation.3 | loop fusion | bytes 4194308 | tf_op jit(solution)/shard_map/dynamic_slice | solution.py:247
  14.4 0.0 collective-permute-done.1
  14.5 0.0 collective-permute-done
  14.5 0.1 copy.7
  14.6 1.1 broadcast_in_dim.6
  15.7 13.0 %all-to-all-start = ((bf16[16,128,256]{2,1,0:T(8,128)(2,1)}), bf16[16,128,256]{2,1,0:T(8,128)(2,1)S(1)}, u32[]{:S(2)}, u32[]{:S(2)}) async-start(bf16[16,128,256]{2,1,0:T(8,128)(2,1)} %broadcast_in_dim.6), calls=%async_computation | async-start | bytes 2097152 | tf_op jit(solution)/shard_map/all_to_all | solution.py:16
  28.7 3.2 %collective-permute-start.2 = (bf16[2,256,256]{2,1,0:T(8,128)(2,1)S(1)}, bf16[2,256,256]{2,1,0:T(8,128)(2,1)S(1)}, u32[]{:S(2)}, u32[]{:S(2)}) collective-permute-start(bf16[2,256,256]{2,1,0:T(8,128)(2,1)S(1)} %pad_maximum_fusion.refs_0_), channel_id=1, source_target_pairs={{0,128},{128,256},{256,384},{384,0},{1,129},{129,257},{257,385},{3... | collective-permute-start | bytes 786440 | tf_op jit(solution)/shard_map/ppermute | solution.py:24
  31.9 4.5 %collective-permute-start.3 = (bf16[2,256,256]{2,1,0:T(8,128)(2,1)S(1)}, bf16[2,256,256]{2,1,0:T(8,128)(2,1)S(1)}, u32[]{:S(2)}, u32[]{:S(2)}) collective-permute-start(bf16[2,256,256]{2,1,0:T(8,128)(2,1)S(1)} %pad_maximum_fusion.refs_0_), channel_id=1, source_target_pairs={{0,256},{128,384},{256,0},{384,128},{1,257},{129,385},{257,1},{385... | collective-permute-start | bytes 786440 | tf_op jit(solution)/shard_map/ppermute | solution.py:24
  36.4 3.0 %collective-permute-start.4 = (bf16[2,256,256]{2,1,0:T(8,128)(2,1)S(1)}, bf16[2,256,256]{2,1,0:T(8,128)(2,1)S(1)}, u32[]{:S(2)}, u32[]{:S(2)}) collective-permute-start(bf16[2,256,256]{2,1,0:T(8,128)(2,1)S(1)} %pad_maximum_fusion.refs_0_), channel_id=1, source_target_pairs={{0,384},{128,0},{256,128},{384,256},{1,385},{129,1},{257,129},{385... | collective-permute-start | bytes 786440 | tf_op jit(solution)/shard_map/ppermute | solution.py:24
  39.4 0.1 collective-permute-done.2.refs_1_
  39.5 6.7 %collective-permute-done.3.refs_2_ = bf16[2,256,256]{2,1,0:T(8,128)(2,1)S(1)} collective-permute-done((bf16[2,256,256]{2,1,0:T(8,128)(2,1)S(1)}, bf16[2,256,256]{2,1,0:T(8,128)(2,1)S(1)}, u32[]{:S(2)}, u32[]{:S(2)}) %collective-permute-start.3) | collective-permute-done | bytes 262176 | tf_op jit(solution)/shard_map/ppermute | solution.py:24
  46.2 1.1 collective-permute-done.4.refs_3_
  47.3 8.7 %all-to-all-done = bf16[16,128,256]{2,1,0:T(8,128)(2,1)S(1)} async-done(((bf16[16,128,256]{2,1,0:T(8,128)(2,1)}), bf16[16,128,256]{2,1,0:T(8,128)(2,1)S(1)}, u32[]{:S(2)}, u32[]{:S(2)}) %all-to-all-start) | async-done | bytes 1048608 | tf_op jit(solution)/shard_map/all_to_all | solution.py:16
  56.0 0.4 shard_map.65
  56.4 0.0 copy-start.5
  56.4 3.4 %collective-permute-start.5 = (f32[512,256]{1,0:T(8,128)S(1)}, f32[512,256]{1,0:T(8,128)S(1)}, u32[]{:S(2)}, u32[]{:S(2)}) collective-permute-start(f32[512,256]{1,0:T(8,128)S(1)} %shard_map.65), channel_id=1, source_target_pairs={{0,1},{1,0},{2,3},{3,2},{4,5},{5,4},{6,7},{7,6},{8,9},{9,8},{10,11... | collective-permute-start | bytes 1572872 | tf_op jit(solution)/shard_map/ppermute | solution.py:24
  59.9 0.4 shard_map.64.kept
  60.4 0.0 copy-start
  60.4 1.1 collective-permute-done.5.received
  61.4 0.2 shard_map.66
  61.6 0.0 copy-done.5
  61.6 2.3 %collective-permute-start.6 = (bf16[256,4096]{1,0:T(8,128)(2,1)S(1)}, bf16[256,4096]{1,0:T(8,128)(2,1)S(1)}, u32[]{:S(2)}, u32[]{:S(2)}) collective-permute-start(bf16[256,4096]{1,0:T(8,128)(2,1)S(1)} %copy-done.5), channel_id=1, source_target_pairs={{0,1},{1,0},{2,3},{3,2},{4,5},{5,4},{6,7},{7,6},{8,9},{9,8},{10,11... | collective-permute-start | bytes 6291464 | tf_op jit(solution)/shard_map/ppermute | solution.py:24
  64.0 22.8 %all_to_all.30 = f16[4,136,256]{2,1,0:T(8,128)(2,1)S(1)} all-to-all(f16[4,136,256]{2,1,0:T(8,128)(2,1)S(1)} %convert_element_type.6), channel_id=1, replica_groups=mesh['y'=4,'zh'=4,'x'=4,'zl'=4,'core'=2] {'zh'}, dimensions={0} | all-to-all | bytes 557056 | tf_op jit(solution)/shard_map/all_to_all | solution.py:16
  86.9 0.1 shard_map.67
  86.9 2.8 %all-gather = bf16[256,256]{1,0:T(8,128)(2,1)S(1)} all-gather(bf16[128,256]{1,0:T(8,128)(2,1)S(1)} %shard_map.67), channel_id=2, replica_groups=mesh['y'=4,'zh'=4,'x'=4,'zl'=4,'core'=2] {'core'}, dimensions={0}, use_global_device_ids=true | all-gather | bytes 196608 | tf_op jit(solution)/shard_map/all_gather | solution.py:266
  89.7 0.0 collective-permute-done.6.their_directions.directions
  89.7 0.0 copy-done
  89.7 1.6 %shard_map.68 = bf16[4,4,128,256]{3,2,1,0:T(8,128)(2,1)S(1)} custom-call(s32[1]{0:T(128)} %bitcast.half, bf16[2,128,256]{2,1,0:T(8,128)(2,1)S(1)} %bitcast.16, bf16[256,8192]{1,0:T(8,128)(2,1)S(1)} %copy-done, bf16[256,4096]{1,0:T(8,128)(2,1)S(1)} %collective-permute-done.6.their_directions.directions), custom_call_target="tpu_custom_call" | custom-call | flops 536870912 | bytes 4194304 | tf_op jit(solution)/shard_map/pallas_call | solution.py:127
  91.3 0.0 copy-start.2
  91.3 0.0 copy-start.3
  91.3 0.0 copy-start.4
  91.3 17.2 %all_to_all.31.parts = bf16[4,4,128,256]{3,2,1,0:T(8,128)(2,1)S(1)} all-to-all(bf16[4,4,128,256]{3,2,1,0:T(8,128)(2,1)S(1)} %shard_map.68), channel_id=1, replica_groups=mesh['y'=4,'zh'=4,'x'=4,'zl'=4,'core'=2] {'x'}, dimensions={0} | all-to-all | bytes 2097152 | tf_op jit(solution)/shard_map/all_to_all | solution.py:16
  108.5 0.8 shard_map.69
  109.4 4.2 %all-to-all-start.3 = ((bf16[4,128,256]{2,1,0:T(8,128)(2,1)}), bf16[4,128,256]{2,1,0:T(8,128)(2,1)S(1)}, u32[]{:S(2)}, u32[]{:S(2)}) async-start(bf16[4,128,256]{2,1,0:T(8,128)(2,1)} %shard_map.69), calls=%async_computation.3 | async-start | bytes 524288 | tf_op jit(solution)/shard_map/all_to_all | solution.py:16
  113.5 5.7 %all-to-all-done.3.parts = bf16[4,128,256]{2,1,0:T(8,128)(2,1)S(1)} async-done(((bf16[4,128,256]{2,1,0:T(8,128)(2,1)}), bf16[4,128,256]{2,1,0:T(8,128)(2,1)S(1)}, u32[]{:S(2)}, u32[]{:S(2)}) %all-to-all-start.3) | async-done | bytes 262176 | tf_op jit(solution)/shard_map/all_to_all | solution.py:16
  119.2 0.0 copy-done.2
  119.2 0.0 copy-done.3
  119.2 0.0 copy-done.4
  119.2 0.7 shard_map.70
  120.0 10.6 %all_to_all.32 = bf16[4,256,128]{2,1,0:T(8,128)(2,1)S(1)} all-to-all(bf16[4,256,128]{2,1,0:T(8,128)(2,1)S(1)} %broadcast_in_dim.7), channel_id=1, replica_groups=mesh['y'=4,'zh'=4,'x'=4,'zl'=4,'core'=2] {'zl'}, dimensions={0} | all-to-all | bytes 524288 | tf_op jit(solution)/shard_map/all_to_all | solution.py:16
  130.6 0.2 broadcast_in_dim.8
  130.8 0.0 copy-start.1
  130.8 13.9 %all_to_all.33 = bf16[4,4,256,128]{3,2,1,0:T(8,128)(2,1)S(1)} all-to-all(bf16[4,4,256,128]{3,2,1,0:T(8,128)(2,1)S(1)} %broadcast_in_dim.8), channel_id=1, replica_groups=mesh['y'=4,'zh'=4,'x'=4,'zl'=4,'core'=2] {'x'}, dimensions={0} | all-to-all | bytes 2097152 | tf_op jit(solution)/shard_map/all_to_all | solution.py:16
  144.7 1.4 shard_map.72
  146.0 6.8 %collective-permute-start.7 = (f32[256,128]{1,0:T(8,128)S(1)}, f32[256,128]{1,0:T(8,128)S(1)}, u32[]{:S(2)}, u32[]{:S(2)}) collective-permute-start(f32[256,128]{1,0:T(8,128)S(1)} %shard_map.72), channel_id=1, source_target_pairs={{0,1},{1,0},{2,3},{3,2},{4,5},{5,4},{6,7},{7,6},{8,9},{9,8},{10,11... | collective-permute-start | bytes 393224 | tf_op jit(solution)/shard_map/ppermute | solution.py:24
  152.8 0.0 copy-done.1
  152.8 1.4 shard_map.71
  154.2 0.0 collective-permute-done.7
  154.2 0.7 add.23
  (4 shorter events, 0.1 us)
Async XLA Ops:
  0.0 14.5 %collective-permute-start = (bf16[128,256]{0,1:T(8,128)(2,1)}, bf16[128,256]{0,1:T(8,128)(2,1)S(1)}, u32[]{:S(2)}, u32[]{:S(2)}) collective-permute-start(bf16[128,256]{0,1:T(8,128)(2,1)} %bitcast.20), channel_id=1, source_target_pairs={{0,0},{2,32},{4,64},{6,96},{32,2},{34,34},{36,66},{38,98},{64,4},{... | collective-permute-start | bytes 196616 | tf_op jit(solution)/shard_map/ppermute | solution.py:246
  2.5 12.0 %collective-permute-start.1 = (bf16[256,256]{1,0:T(8,128)(2,1)S(1)}, bf16[256,256]{1,0:T(8,128)(2,1)S(1)}, u32[]{:S(2)}, u32[]{:S(2)}) collective-permute-start(bf16[256,256]{1,0:T(8,128)(2,1)S(1)} %get-tuple-element.26), channel_id=1, source_target_pairs={{0,1},{1,0},{2,3},{3,2},{4,5},{5,4},{6,7},{7,6},{8,9},{9,8},{10,11... | collective-permute-start | bytes 393224 | tf_op jit(solution)/shard_map/ppermute | solution.py:24
  15.7 40.3 %all-to-all-start = ((bf16[16,128,256]{2,1,0:T(8,128)(2,1)}), bf16[16,128,256]{2,1,0:T(8,128)(2,1)S(1)}, u32[]{:S(2)}, u32[]{:S(2)}) async-start(bf16[16,128,256]{2,1,0:T(8,128)(2,1)} %broadcast_in_dim.6), calls=%async_computation | async-start | bytes 2097152 | tf_op jit(solution)/shard_map/all_to_all | solution.py:16
  28.7 10.9 %collective-permute-start.2 = (bf16[2,256,256]{2,1,0:T(8,128)(2,1)S(1)}, bf16[2,256,256]{2,1,0:T(8,128)(2,1)S(1)}, u32[]{:S(2)}, u32[]{:S(2)}) collective-permute-start(bf16[2,256,256]{2,1,0:T(8,128)(2,1)S(1)} %pad_maximum_fusion.refs_0_), channel_id=1, source_target_pairs={{0,128},{128,256},{256,384},{384,0},{1,129},{129,257},{257,385},{3... | collective-permute-start | bytes 786440 | tf_op jit(solution)/shard_map/ppermute | solution.py:24
  31.9 14.4 %collective-permute-start.3 = (bf16[2,256,256]{2,1,0:T(8,128)(2,1)S(1)}, bf16[2,256,256]{2,1,0:T(8,128)(2,1)S(1)}, u32[]{:S(2)}, u32[]{:S(2)}) collective-permute-start(bf16[2,256,256]{2,1,0:T(8,128)(2,1)S(1)} %pad_maximum_fusion.refs_0_), channel_id=1, source_target_pairs={{0,256},{128,384},{256,0},{384,128},{1,257},{129,385},{257,1},{385... | collective-permute-start | bytes 786440 | tf_op jit(solution)/shard_map/ppermute | solution.py:24
  36.4 10.9 %collective-permute-start.4 = (bf16[2,256,256]{2,1,0:T(8,128)(2,1)S(1)}, bf16[2,256,256]{2,1,0:T(8,128)(2,1)S(1)}, u32[]{:S(2)}, u32[]{:S(2)}) collective-permute-start(bf16[2,256,256]{2,1,0:T(8,128)(2,1)S(1)} %pad_maximum_fusion.refs_0_), channel_id=1, source_target_pairs={{0,384},{128,0},{256,128},{384,256},{1,385},{129,1},{257,129},{385... | collective-permute-start | bytes 786440 | tf_op jit(solution)/shard_map/ppermute | solution.py:24
  56.4 5.2 %copy-start.5 = (bf16[256,4096]{1,0:T(8,128)(2,1)S(1)}, bf16[256,4096]{1,0:T(8,128)(2,1)}, u32[]{:S(2)}) copy-start(bf16[256,4096]{1,0:T(8,128)(2,1)} %constant_dynamic-slice_fusion.1) | copy-start | bytes 6291460
  56.4 5.0 %collective-permute-start.5 = (f32[512,256]{1,0:T(8,128)S(1)}, f32[512,256]{1,0:T(8,128)S(1)}, u32[]{:S(2)}, u32[]{:S(2)}) collective-permute-start(f32[512,256]{1,0:T(8,128)S(1)} %shard_map.65), channel_id=1, source_target_pairs={{0,1},{1,0},{2,3},{3,2},{4,5},{5,4},{6,7},{7,6},{8,9},{9,8},{10,11... | collective-permute-start | bytes 1572872 | tf_op jit(solution)/shard_map/ppermute | solution.py:24
  60.4 29.3 %copy-start = (bf16[256,8192]{1,0:T(8,128)(2,1)S(1)}, bf16[256,8192]{1,0:T(8,128)(2,1)}, u32[]{:S(2)}) copy-start(bf16[256,8192]{1,0:T(8,128)(2,1)} %directions.3) | copy-start | bytes 12582916
  61.6 28.0 %collective-permute-start.6 = (bf16[256,4096]{1,0:T(8,128)(2,1)S(1)}, bf16[256,4096]{1,0:T(8,128)(2,1)S(1)}, u32[]{:S(2)}, u32[]{:S(2)}) collective-permute-start(bf16[256,4096]{1,0:T(8,128)(2,1)S(1)} %copy-done.5), channel_id=1, source_target_pairs={{0,1},{1,0},{2,3},{3,2},{4,5},{5,4},{6,7},{7,6},{8,9},{9,8},{10,11... | collective-permute-start | bytes 6291464 | tf_op jit(solution)/shard_map/ppermute | solution.py:24
  91.3 27.9 %copy-start.2 = (f32[8192]{0:T(1024)S(1)}, f32[8192]{0:T(1024)}, u32[]{:S(2)}) copy-start(f32[8192]{0:T(1024)} %param.9) | copy-start | bytes 98308
  91.3 27.9 %copy-start.3 = (s32[128]{0:T(128)S(1)}, s32[128]{0:T(128)}, u32[]{:S(2)}) copy-start(s32[128]{0:T(128)} %param.11) | copy-start | bytes 1540
  91.3 27.9 %copy-start.4 = (f32[16]{0:T(128)S(1)}, f32[16]{0:T(128)}, u32[]{:S(2)}) copy-start(f32[16]{0:T(128)} %grid_values.1) | copy-start | bytes 196
  109.4 9.8 %all-to-all-start.3 = ((bf16[4,128,256]{2,1,0:T(8,128)(2,1)}), bf16[4,128,256]{2,1,0:T(8,128)(2,1)S(1)}, u32[]{:S(2)}, u32[]{:S(2)}) async-start(bf16[4,128,256]{2,1,0:T(8,128)(2,1)} %shard_map.69), calls=%async_computation.3 | async-start | bytes 524288 | tf_op jit(solution)/shard_map/all_to_all | solution.py:16
  130.8 22.1 %copy-start.1 = (bf16[256,8192]{1,0:T(8,128)(2,1)S(1)}, bf16[256,8192]{1,0:T(8,128)(2,1)}, u32[]{:S(2)}) copy-start(bf16[256,8192]{1,0:T(8,128)(2,1)} %directions.3) | copy-start | bytes 12582916
  146.0 8.2 %collective-permute-start.7 = (f32[256,128]{1,0:T(8,128)S(1)}, f32[256,128]{1,0:T(8,128)S(1)}, u32[]{:S(2)}, u32[]{:S(2)}) collective-permute-start(f32[256,128]{1,0:T(8,128)S(1)} %shard_map.72), channel_id=1, source_target_pairs={{0,1},{1,0},{2,3},{3,2},{4,5},{5,4},{6,7},{7,6},{8,9},{9,8},{10,11... | collective-permute-start | bytes 393224 | tf_op jit(solution)/shard_map/ppermute | solution.py:24

commit v5 on v4

--- a/solution.py
+++ b/solution.py
@@ -258,7 +258,6 @@
     kept = cross_products(0, y, signals, features)
     cross = scaled(kept, received, nzh, 2 * half * ny * nzh)
 
-    cross, given = lax.optimization_barrier((cross, given))
     their_directions = shift(given, "core", 2, 1)
     parts = exchange(cross.astype(F16), "zh").astype(F32)
 

time: 156 us -> 155 us (level)
  waiting for transfers between devices: 23.3 us -> 20.1 us
  Pallas kernels: 7.1 us -> 9.29 us
    all_to_all x2, waiting for transfers between devices: 14.4 us -> 12 us  [exchange(): return lax.all_to_all(blocks, axis, 0, 0, tiled=True)]
    pallas_call x2, Pallas kernels: 0.88 us -> 3.09 us  [cross_products(): pl.pallas_call(functools.partial(cross_kernel, ny, which), out_shape=jax....]
  transfers between devices with their start and end apart: 10 -> 10, of which waited for: 6 -> 5; matrix products, arithmetic and copies ran while one was open for 3% -> 3% of each run, Pallas kernels for 1% -> 3%
where the time goes in v5:
time: 155 us; the launch traced here: 154 us
  blocking collectives  67.6 us (44%)
  starting transfers between devices  50.4 us (33%)
  waiting for transfers between devices  20.1 us (13%)
  Pallas kernels  9.29 us (6%)
  local copies, waits for them, and re-layouts  5.58 us (4%)
    all_to_all x4, blocking collectives, exchange(): return lax.all_to_all(blocks, axis, 0, 0, tiled=True)  64.8 us
    ppermute x7, starting transfers between devices, shift(): lax.ppermute(block, axis, [(i, (i + by) % size) for i in range(size)])  31.8 us
    all_to_all x2, starting transfers between devices, exchange(): return lax.all_to_all(blocks, axis, 0, 0, tiled=True)  17.2 us
    all_to_all x2, waiting for transfers between devices, exchange(): return lax.all_to_all(blocks, axis, 0, 0, tiled=True)  12 us
    ppermute x7, waiting for transfers between devices, shift(): lax.ppermute(block, axis, [(i, (i + by) % size) for i in range(size)])  8.11 us
    dynamic_slice x1, local copies, waits for them, and re-layouts, per_device(): lax.dynamic_slice_in_dim(spectral_directions, (1 - core) * (width // 2),...  3.16 us
  transfers between devices with their start and end apart: 10, of which 5 were waited for; matrix products, arithmetic and copies ran while one was open for 3% of the time, Pallas kernels for 3%

profile of v5, /device:TPU:1, one launch (start us, length us, event | category | flops | bytes accessed | tf_op | source)
XLA Modules:
  0.0 154.0 jit_solution(5275551235111373624)
XLA Ops:
  0.0 1.5 collective-permute-start
  1.5 1.0 dynamic-slice_bitcast_fusion
  2.5 8.8 %collective-permute-start.1 = (bf16[256,256]{1,0:T(8,128)(2,1)S(1)}, bf16[256,256]{1,0:T(8,128)(2,1)S(1)}, u32[]{:S(2)}, u32[]{:S(2)}) collective-permute-start(bf16[256,256]{1,0:T(8,128)(2,1)S(1)} %get-tuple-element.22), channel_id=1, source_target_pairs={{0,1},{1,0},{2,3},{3,2},{4,5},{5,4},{6,7},{7,6},{8,9},{9,8},{10,11... | collective-permute-start | bytes 393224 | tf_op jit(solution)/shard_map/ppermute | solution.py:24
  11.3 3.2 %constant_dynamic-slice_fusion.1 = bf16[256,4096]{1,0:T(8,128)(2,1)} fusion(bf16[256,8192]{1,0:T(8,128)(2,1)} %directions.3, s32[]{:T(128)S(6)} %select_n.9), kind=kLoop, calls=%fused_computation.3 | loop fusion | bytes 4194308 | tf_op jit(solution)/shard_map/dynamic_slice | solution.py:247
  14.4 0.0 collective-permute-done.1
  14.5 0.0 collective-permute-done
  14.5 0.1 copy.7
  14.6 1.1 broadcast_in_dim.6
  15.7 13.0 %all-to-all-start = ((bf16[16,128,256]{2,1,0:T(8,128)(2,1)}), bf16[16,128,256]{2,1,0:T(8,128)(2,1)S(1)}, u32[]{:S(2)}, u32[]{:S(2)}) async-start(bf16[16,128,256]{2,1,0:T(8,128)(2,1)} %broadcast_in_dim.6), calls=%async_computation | async-start | bytes 2097152 | tf_op jit(solution)/shard_map/all_to_all | solution.py:16
  28.7 2.2 %collective-permute-start.6 = (bf16[256,4096]{1,0:T(8,128)(2,1)}, bf16[256,4096]{1,0:T(8,128)(2,1)S(1)}, u32[]{:S(2)}, u32[]{:S(2)}) collective-permute-start(bf16[256,4096]{1,0:T(8,128)(2,1)} %constant_dynamic-slice_fusion.1), channel_id=1, source_target_pairs={{0,1},{1,0},{2,3},{3,2},{4,5},{5,4},{6,7},{7,6},{8,9},{9,8},{10,11... | collective-permute-start | bytes 6291464 | tf_op jit(solution)/shard_map/ppermute | solution.py:24
  30.9 3.2 %collective-permute-start.2 = (bf16[2,256,256]{2,1,0:T(8,128)(2,1)S(1)}, bf16[2,256,256]{2,1,0:T(8,128)(2,1)}, u32[]{:S(2)}, u32[]{:S(2)}) collective-permute-start(bf16[2,256,256]{2,1,0:T(8,128)(2,1)S(1)} %pad_maximum_fusion.refs_0_), channel_id=1, source_target_pairs={{0,128},{128,256},{256,384},{384,0},{1,129},{129,257},{257,385},{3... | collective-permute-start | bytes 786440 | tf_op jit(solution)/shard_map/ppermute | solution.py:24
  34.1 4.5 %collective-permute-start.3 = (bf16[2,256,256]{2,1,0:T(8,128)(2,1)S(1)}, bf16[2,256,256]{2,1,0:T(8,128)(2,1)}, u32[]{:S(2)}, u32[]{:S(2)}) collective-permute-start(bf16[2,256,256]{2,1,0:T(8,128)(2,1)S(1)} %pad_maximum_fusion.refs_0_), channel_id=1, source_target_pairs={{0,256},{128,384},{256,0},{384,128},{1,257},{129,385},{257,1},{385... | collective-permute-start | bytes 786440 | tf_op jit(solution)/shard_map/ppermute | solution.py:24
  38.6 3.0 %collective-permute-start.4 = (bf16[2,256,256]{2,1,0:T(8,128)(2,1)S(1)}, bf16[2,256,256]{2,1,0:T(8,128)(2,1)}, u32[]{:S(2)}, u32[]{:S(2)}) collective-permute-start(bf16[2,256,256]{2,1,0:T(8,128)(2,1)S(1)} %pad_maximum_fusion.refs_0_), channel_id=1, source_target_pairs={{0,384},{128,0},{256,128},{384,256},{1,385},{129,1},{257,129},{385... | collective-permute-start | bytes 786440 | tf_op jit(solution)/shard_map/ppermute | solution.py:24
  41.6 0.3 collective-permute-done.2.refs_1_
  41.9 6.7 %collective-permute-done.3.refs_2_ = bf16[2,256,256]{2,1,0:T(8,128)(2,1)} collective-permute-done((bf16[2,256,256]{2,1,0:T(8,128)(2,1)S(1)}, bf16[2,256,256]{2,1,0:T(8,128)(2,1)}, u32[]{:S(2)}, u32[]{:S(2)}) %collective-permute-start.3) | collective-permute-done | bytes 262176 | tf_op jit(solution)/shard_map/ppermute | solution.py:24
  48.6 1.1 collective-permute-done.4.refs_3_
  49.7 6.3 %all-to-all-done = bf16[16,128,256]{2,1,0:T(8,128)(2,1)S(1)} async-done(((bf16[16,128,256]{2,1,0:T(8,128)(2,1)}), bf16[16,128,256]{2,1,0:T(8,128)(2,1)S(1)}, u32[]{:S(2)}, u32[]{:S(2)}) %all-to-all-start) | async-done | bytes 1048608 | tf_op jit(solution)/shard_map/all_to_all | solution.py:16
  56.0 1.5 %shard_map.65 = f32[512,256]{1,0:T(8,128)S(1)} custom-call(s32[1]{0:T(128)} %bitcast.2.y, bf16[4,4,128,256]{3,2,1,0:T(8,128)(2,1)S(1)} %bitcast.12, bf16[2,256,256]{2,1,0:T(8,128)(2,1)S(1)} %pad_maximum_fusion.refs_0_, bf16[2,256,256]{2,1,0:T(8,128)(2,1)} %collective-permute-done.2.refs_1_, bf16[2,256,256]{2,1,0:T(8,128)(2,1)} %collective-permute-done.3.refs_2_, ...), custom_call_target="tpu_custom_call" | custom-call | flops 268435456 | bytes 4194304 | tf_op jit(solution)/shard_map/pallas_call | solution.py:45
  57.5 3.3 %collective-permute-start.5 = (f32[512,256]{1,0:T(8,128)S(1)}, f32[512,256]{1,0:T(8,128)S(1)}, u32[]{:S(2)}, u32[]{:S(2)}) collective-permute-start(f32[512,256]{1,0:T(8,128)S(1)} %shard_map.65), channel_id=1, source_target_pairs={{0,1},{1,0},{2,3},{3,2},{4,5},{5,4},{6,7},{7,6},{8,9},{9,8},{10,11... | collective-permute-start | bytes 1572872 | tf_op jit(solution)/shard_map/ppermute | solution.py:24
  60.9 1.5 %shard_map.64.kept = f32[512,256]{1,0:T(8,128)S(1)} custom-call(s32[1]{0:T(128)} %bitcast.2.y, bf16[4,4,128,256]{3,2,1,0:T(8,128)(2,1)S(1)} %bitcast.13, bf16[2,256,256]{2,1,0:T(8,128)(2,1)S(1)} %pad_maximum_fusion.refs_0_, bf16[2,256,256]{2,1,0:T(8,128)(2,1)} %collective-permute-done.2.refs_1_, bf16[2,256,256]{2,1,0:T(8,128)(2,1)} %collective-permute-done.3.refs_2_, ...), custom_call_target="tpu_custom_call" | custom-call | flops 268435456 | bytes 4194304 | tf_op jit(solution)/shard_map/pallas_call | solution.py:45
  62.4 0.0 copy-start
  62.4 0.0 collective-permute-done.5.received
  62.4 0.2 shard_map.66
  62.7 23.1 %all_to_all.30 = f16[4,136,256]{2,1,0:T(8,128)(2,1)S(1)} all-to-all(f16[4,136,256]{2,1,0:T(8,128)(2,1)S(1)} %convert_element_type.6), channel_id=1, replica_groups=mesh['y'=4,'zh'=4,'x'=4,'zl'=4,'core'=2] {'zh'}, dimensions={0} | all-to-all | bytes 557056 | tf_op jit(solution)/shard_map/all_to_all | solution.py:16
  85.8 0.1 shard_map.67
  85.9 2.7 %all-gather = bf16[256,256]{1,0:T(8,128)(2,1)S(1)} all-gather(bf16[128,256]{1,0:T(8,128)(2,1)S(1)} %shard_map.67), channel_id=2, replica_groups=mesh['y'=4,'zh'=4,'x'=4,'zl'=4,'core'=2] {'core'}, dimensions={0}, use_global_device_ids=true | all-gather | bytes 196608 | tf_op jit(solution)/shard_map/all_gather | solution.py:265
  88.6 0.0 collective-permute-done.6.their_directions.directions
  88.6 0.0 copy-done
  88.6 1.6 %shard_map.68 = bf16[4,4,128,256]{3,2,1,0:T(8,128)(2,1)S(1)} custom-call(s32[1]{0:T(128)} %bitcast.half, bf16[2,128,256]{2,1,0:T(8,128)(2,1)S(1)} %bitcast.16, bf16[256,8192]{1,0:T(8,128)(2,1)S(1)} %copy-done, bf16[256,4096]{1,0:T(8,128)(2,1)S(1)} %collective-permute-done.6.their_directions.directions), custom_call_target="tpu_custom_call" | custom-call | flops 536870912 | bytes 4194304 | tf_op jit(solution)/shard_map/pallas_call | solution.py:127
  90.3 0.0 copy-start.2
  90.3 0.0 copy-start.3
  90.3 0.0 copy-start.4
  90.3 17.2 %all_to_all.31.parts = bf16[4,4,128,256]{3,2,1,0:T(8,128)(2,1)S(1)} all-to-all(bf16[4,4,128,256]{3,2,1,0:T(8,128)(2,1)S(1)} %shard_map.68), channel_id=1, replica_groups=mesh['y'=4,'zh'=4,'x'=4,'zl'=4,'core'=2] {'x'}, dimensions={0} | all-to-all | bytes 2097152 | tf_op jit(solution)/shard_map/all_to_all | solution.py:16
  107.5 0.8 shard_map.69
  108.4 4.2 %all-to-all-start.3 = ((bf16[4,128,256]{2,1,0:T(8,128)(2,1)}), bf16[4,128,256]{2,1,0:T(8,128)(2,1)S(1)}, u32[]{:S(2)}, u32[]{:S(2)}) async-start(bf16[4,128,256]{2,1,0:T(8,128)(2,1)} %shard_map.69), calls=%async_computation.3 | async-start | bytes 524288 | tf_op jit(solution)/shard_map/all_to_all | solution.py:16
  112.6 5.7 %all-to-all-done.3.parts = bf16[4,128,256]{2,1,0:T(8,128)(2,1)S(1)} async-done(((bf16[4,128,256]{2,1,0:T(8,128)(2,1)}), bf16[4,128,256]{2,1,0:T(8,128)(2,1)S(1)}, u32[]{:S(2)}, u32[]{:S(2)}) %all-to-all-start.3) | async-done | bytes 262176 | tf_op jit(solution)/shard_map/all_to_all | solution.py:16
  118.2 0.0 copy-done.2
  118.2 0.0 copy-done.3
  118.2 0.0 copy-done.4
  118.2 0.7 shard_map.70
  119.0 10.6 %all_to_all.32 = bf16[4,256,128]{2,1,0:T(8,128)(2,1)S(1)} all-to-all(bf16[4,256,128]{2,1,0:T(8,128)(2,1)S(1)} %broadcast_in_dim.7), channel_id=1, replica_groups=mesh['y'=4,'zh'=4,'x'=4,'zl'=4,'core'=2] {'zl'}, dimensions={0} | all-to-all | bytes 524288 | tf_op jit(solution)/shard_map/all_to_all | solution.py:16
  129.6 0.2 broadcast_in_dim.8
  129.8 0.0 copy-start.1
  129.8 13.9 %all_to_all.33 = bf16[4,4,256,128]{3,2,1,0:T(8,128)(2,1)S(1)} all-to-all(bf16[4,4,256,128]{3,2,1,0:T(8,128)(2,1)S(1)} %broadcast_in_dim.8), channel_id=1, replica_groups=mesh['y'=4,'zh'=4,'x'=4,'zl'=4,'core'=2] {'x'}, dimensions={0} | all-to-all | bytes 2097152 | tf_op jit(solution)/shard_map/all_to_all | solution.py:16
  143.7 1.4 shard_map.72
  145.1 6.8 %collective-permute-start.7 = (f32[256,128]{1,0:T(8,128)S(1)}, f32[256,128]{1,0:T(8,128)S(1)}, u32[]{:S(2)}, u32[]{:S(2)}) collective-permute-start(f32[256,128]{1,0:T(8,128)S(1)} %shard_map.72), channel_id=1, source_target_pairs={{0,1},{1,0},{2,3},{3,2},{4,5},{5,4},{6,7},{7,6},{8,9},{9,8},{10,11... | collective-permute-start | bytes 393224 | tf_op jit(solution)/shard_map/ppermute | solution.py:24
  151.9 0.0 copy-done.1
  151.9 1.4 shard_map.71
  153.3 0.0 collective-permute-done.7
  153.3 0.7 add.23
  (4 shorter events, 0.1 us)
Async XLA Ops:
  0.0 14.5 %collective-permute-start = (bf16[128,256]{0,1:T(8,128)(2,1)}, bf16[128,256]{0,1:T(8,128)(2,1)S(1)}, u32[]{:S(2)}, u32[]{:S(2)}) collective-permute-start(bf16[128,256]{0,1:T(8,128)(2,1)} %bitcast.20), channel_id=1, source_target_pairs={{0,0},{2,32},{4,64},{6,96},{32,2},{34,34},{36,66},{38,98},{64,4},{... | collective-permute-start | bytes 196616 | tf_op jit(solution)/shard_map/ppermute | solution.py:246
  2.5 12.0 %collective-permute-start.1 = (bf16[256,256]{1,0:T(8,128)(2,1)S(1)}, bf16[256,256]{1,0:T(8,128)(2,1)S(1)}, u32[]{:S(2)}, u32[]{:S(2)}) collective-permute-start(bf16[256,256]{1,0:T(8,128)(2,1)S(1)} %get-tuple-element.22), channel_id=1, source_target_pairs={{0,1},{1,0},{2,3},{3,2},{4,5},{5,4},{6,7},{7,6},{8,9},{9,8},{10,11... | collective-permute-start | bytes 393224 | tf_op jit(solution)/shard_map/ppermute | solution.py:24
  15.7 40.3 %all-to-all-start = ((bf16[16,128,256]{2,1,0:T(8,128)(2,1)}), bf16[16,128,256]{2,1,0:T(8,128)(2,1)S(1)}, u32[]{:S(2)}, u32[]{:S(2)}) async-start(bf16[16,128,256]{2,1,0:T(8,128)(2,1)} %broadcast_in_dim.6), calls=%async_computation | async-start | bytes 2097152 | tf_op jit(solution)/shard_map/all_to_all | solution.py:16
  28.7 60.0 %collective-permute-start.6 = (bf16[256,4096]{1,0:T(8,128)(2,1)}, bf16[256,4096]{1,0:T(8,128)(2,1)S(1)}, u32[]{:S(2)}, u32[]{:S(2)}) collective-permute-start(bf16[256,4096]{1,0:T(8,128)(2,1)} %constant_dynamic-slice_fusion.1), channel_id=1, source_target_pairs={{0,1},{1,0},{2,3},{3,2},{4,5},{5,4},{6,7},{7,6},{8,9},{9,8},{10,11... | collective-permute-start | bytes 6291464 | tf_op jit(solution)/shard_map/ppermute | solution.py:24
  30.9 11.1 %collective-permute-start.2 = (bf16[2,256,256]{2,1,0:T(8,128)(2,1)S(1)}, bf16[2,256,256]{2,1,0:T(8,128)(2,1)}, u32[]{:S(2)}, u32[]{:S(2)}) collective-permute-start(bf16[2,256,256]{2,1,0:T(8,128)(2,1)S(1)} %pad_maximum_fusion.refs_0_), channel_id=1, source_target_pairs={{0,128},{128,256},{256,384},{384,0},{1,129},{129,257},{257,385},{3... | collective-permute-start | bytes 786440 | tf_op jit(solution)/shard_map/ppermute | solution.py:24
  34.1 14.6 %collective-permute-start.3 = (bf16[2,256,256]{2,1,0:T(8,128)(2,1)S(1)}, bf16[2,256,256]{2,1,0:T(8,128)(2,1)}, u32[]{:S(2)}, u32[]{:S(2)}) collective-permute-start(bf16[2,256,256]{2,1,0:T(8,128)(2,1)S(1)} %pad_maximum_fusion.refs_0_), channel_id=1, source_target_pairs={{0,256},{128,384},{256,0},{384,128},{1,257},{129,385},{257,1},{385... | collective-permute-start | bytes 786440 | tf_op jit(solution)/shard_map/ppermute | solution.py:24
  38.6 11.1 %collective-permute-start.4 = (bf16[2,256,256]{2,1,0:T(8,128)(2,1)S(1)}, bf16[2,256,256]{2,1,0:T(8,128)(2,1)}, u32[]{:S(2)}, u32[]{:S(2)}) collective-permute-start(bf16[2,256,256]{2,1,0:T(8,128)(2,1)S(1)} %pad_maximum_fusion.refs_0_), channel_id=1, source_target_pairs={{0,384},{128,0},{256,128},{384,256},{1,385},{129,1},{257,129},{385... | collective-permute-start | bytes 786440 | tf_op jit(solution)/shard_map/ppermute | solution.py:24
  57.5 4.9 %collective-permute-start.5 = (f32[512,256]{1,0:T(8,128)S(1)}, f32[512,256]{1,0:T(8,128)S(1)}, u32[]{:S(2)}, u32[]{:S(2)}) collective-permute-start(f32[512,256]{1,0:T(8,128)S(1)} %shard_map.65), channel_id=1, source_target_pairs={{0,1},{1,0},{2,3},{3,2},{4,5},{5,4},{6,7},{7,6},{8,9},{9,8},{10,11... | collective-permute-start | bytes 1572872 | tf_op jit(solution)/shard_map/ppermute | solution.py:24
  62.4 26.2 %copy-start = (bf16[256,8192]{1,0:T(8,128)(2,1)S(1)}, bf16[256,8192]{1,0:T(8,128)(2,1)}, u32[]{:S(2)}) copy-start(bf16[256,8192]{1,0:T(8,128)(2,1)} %directions.3) | copy-start | bytes 12582916
  90.3 28.0 %copy-start.2 = (f32[8192]{0:T(1024)S(1)}, f32[8192]{0:T(1024)}, u32[]{:S(2)}) copy-start(f32[8192]{0:T(1024)} %param.9) | copy-start | bytes 98308
  90.3 27.9 %copy-start.3 = (s32[128]{0:T(128)S(1)}, s32[128]{0:T(128)}, u32[]{:S(2)}) copy-start(s32[128]{0:T(128)} %param.11) | copy-start | bytes 1540
  90.3 27.9 %copy-start.4 = (f32[16]{0:T(128)S(1)}, f32[16]{0:T(128)}, u32[]{:S(2)}) copy-start(f32[16]{0:T(128)} %grid_values.1) | copy-start | bytes 196
  108.4 9.9 %all-to-all-start.3 = ((bf16[4,128,256]{2,1,0:T(8,128)(2,1)}), bf16[4,128,256]{2,1,0:T(8,128)(2,1)S(1)}, u32[]{:S(2)}, u32[]{:S(2)}) async-start(bf16[4,128,256]{2,1,0:T(8,128)(2,1)} %shard_map.69), calls=%async_computation.3 | async-start | bytes 524288 | tf_op jit(solution)/shard_map/all_to_all | solution.py:16
  129.8 22.1 %copy-start.1 = (bf16[256,8192]{1,0:T(8,128)(2,1)S(1)}, bf16[256,8192]{1,0:T(8,128)(2,1)}, u32[]{:S(2)}) copy-start(bf16[256,8192]{1,0:T(8,128)(2,1)} %directions.3) | copy-start | bytes 12582916
  145.1 8.2 %collective-permute-start.7 = (f32[256,128]{1,0:T(8,128)S(1)}, f32[256,128]{1,0:T(8,128)S(1)}, u32[]{:S(2)}, u32[]{:S(2)}) collective-permute-start(f32[256,128]{1,0:T(8,128)S(1)} %shard_map.72), channel_id=1, source_target_pairs={{0,1},{1,0},{2,3},{3,2},{4,5},{5,4},{6,7},{7,6},{8,9},{9,8},{10,11... | collective-permute-start | bytes 393224 | tf_op jit(solution)/shard_map/ppermute | solution.py:24

commit v6 on v5

--- a/solution.py
+++ b/solution.py
@@ -197,35 +197,39 @@
     )(which, parts, strengths.reshape(-1, 1, share), slots.reshape(1, voxels), grid_values)
 
 
-def encode_kernel(half, directions, shrunk, out):
+def encode_kernel(half, directions, their_directions, shrunk, own, theirs):
     @pl.when(pl.program_id(0) == 0)
     def _():
-        out[...] = jnp.zeros_like(out)
-
-    out[...] += jnp.dot(directions[...], shrunk[...], preferred_element_type=F32)
-
-
-def encode(half, directions, shrunk, steps=4):
+        own[...] = jnp.zeros_like(own)
+        theirs[...] = jnp.zeros_like(theirs)
+
+    theirs[...] += jnp.dot(their_directions[...], shrunk[...], preferred_element_type=F32)
+    own[...] += jnp.dot(directions[...], shrunk[...], preferred_element_type=F32)
+
+
+def encode(half, directions, their_directions, shrunk, steps=4):
     rows, _ = directions.shape
     depth, voxels = shrunk.shape
     columns = depth // steps
+    flat = pl.BlockSpec((rows, voxels), lambda i, h: (0, 0))
     return pl.pallas_call(
         encode_kernel,
-        out_shape=jax.ShapeDtypeStruct((rows, voxels), F32),
+        out_shape=[jax.ShapeDtypeStruct((rows, voxels), F32)] * 2,
         grid_spec=pltpu.PrefetchScalarGridSpec(
             num_scalar_prefetch=1,
             grid=(steps,),
             in_specs=[
                 pl.BlockSpec((rows, columns), lambda i, h: (0, h[0] * steps + i)),
+                pl.BlockSpec((rows, columns), lambda i, h: (0, i)),
                 pl.BlockSpec((columns, voxels), lambda i, h: (i, 0)),
             ],
-            out_specs=pl.BlockSpec((rows, voxels), lambda i, h: (0, 0)),
-        ),
-        compiler_params=pltpu.CompilerParams(vmem_limit_bytes=16 << 20),
-        cost_estimate=pl.CostEstimate(
-            flops=2 * rows * depth * voxels, bytes_accessed=4 << 20, transcendentals=0
-        ),
-    )(half, directions, shrunk)
+            out_specs=[flat, flat],
+        ),
+        compiler_params=pltpu.CompilerParams(vmem_limit_bytes=16 << 20),
+        cost_estimate=pl.CostEstimate(
+            flops=4 * rows * depth * voxels, bytes_accessed=4 << 20, transcendentals=0
+        ),
+    )(half, directions, their_directions, shrunk)
 
 
 def per_device(
@@ -273,9 +277,9 @@
 
     shrunk = gather(shrunk, "zl", nzl)
     shrunk = gather(shrunk, "x", nx).reshape(width // 2, -1)
-    theirs = encode(jnp.zeros((1,), jnp.int32), their_directions, shrunk)
-    received = shift(theirs, "core", 2, 1)
-    return encode(mine, spectral_directions, shrunk) + received
+    own, theirs = encode(mine, spectral_directions, their_directions, shrunk)
+    theirs = lax.all_gather(theirs, "core", axis=0, tiled=False)
+    return own + lax.dynamic_index_in_dim(theirs, 1 - core, 0, keepdims=False)
 
 
 def solution(mesh):

time: 155 us -> 158 us (1.019)
  waiting for transfers between devices: 20.1 us -> 30.9 us
  blocking collectives: 67.6 us -> 60.5 us
  starting transfers between devices: 50.4 us -> 47.2 us
  local copies, waits for them, and re-layouts: 5.58 us -> 8.75 us
    all_to_all x4 -> x3, blocking collectives: 64.8 us -> 50.9 us  [exchange(): return lax.all_to_all(blocks, axis, 0, 0, tiled=True)]
    all_to_all x2 -> x3, waiting for transfers between devices: 12 us -> 22.8 us  [exchange(): return lax.all_to_all(blocks, axis, 0, 0, tiled=True)]
    all_gather x0 -> x1, blocking collectives: none -> 6.79 us  [per_device(): theirs = lax.all_gather(theirs, 'core', axis=0, tiled=False)]
    ppermute x7 -> x6, starting transfers between devices: 31.8 us -> 25 us  [shift(): lax.ppermute(block, axis, [(i, (i + by) % size) for i in range(size)])]
    all_to_all x2 -> x3, starting transfers between devices: 17.2 us -> 20.7 us  [exchange(): return lax.all_to_all(blocks, axis, 0, 0, tiled=True)]
    unnamed x10, local copies, waits for them, and re-layouts: 0.03 us -> 2.21 us
    ppermute x7 -> x6, waiting for transfers between devices: 8.11 us -> 8.11 us  [shift(): lax.ppermute(block, axis, [(i, (i + by) % size) for i in range(size)])]
  transfers between devices with their start and end apart: 10 -> 10, of which waited for: 5 -> 6; matrix products, arithmetic and copies ran while one was open for 3% -> 3% of each run, Pallas kernels for 3% -> 2%
where the time goes in v6:
time: 158 us; the launch traced here: 157 us
  blocking collectives  60.5 us (38%)
  starting transfers between devices  47.2 us (30%)
  waiting for transfers between devices  30.9 us (20%)
  local copies, waits for them, and re-layouts  8.75 us (6%)
  Pallas kernels  8.59 us (5%)
    all_to_all x3, blocking collectives, exchange(): return lax.all_to_all(blocks, axis, 0, 0, tiled=True)  50.9 us
    ppermute x6, starting transfers between devices, shift(): lax.ppermute(block, axis, [(i, (i + by) % size) for i in range(size)])  25 us
    all_to_all x3, waiting for transfers between devices, exchange(): return lax.all_to_all(blocks, axis, 0, 0, tiled=True)  22.8 us
    all_to_all x3, starting transfers between devices, exchange(): return lax.all_to_all(blocks, axis, 0, 0, tiled=True)  20.7 us
    ppermute x6, waiting for transfers between devices, shift(): lax.ppermute(block, axis, [(i, (i + by) % size) for i in range(size)])  8.11 us
    all_gather x1, blocking collectives, per_device(): theirs = lax.all_gather(theirs, 'core', axis=0, tiled=False)  6.79 us
  transfers between devices with their start and end apart: 10, of which 6 were waited for; matrix products, arithmetic and copies ran while one was open for 3% of the time, Pallas kernels for 2%

profile of v6, /device:TPU:1, one launch (start us, length us, event | category | flops | bytes accessed | tf_op | source)
XLA Modules:
  0.0 156.9 jit_solution(14869837049837116304)
XLA Ops:
  0.0 1.5 collective-permute-start
  1.5 1.0 dynamic-slice_bitcast_fusion
  2.5 8.8 %collective-permute-start.1 = (bf16[256,256]{1,0:T(8,128)(2,1)S(1)}, bf16[256,256]{1,0:T(8,128)(2,1)S(1)}, u32[]{:S(2)}, u32[]{:S(2)}) collective-permute-start(bf16[256,256]{1,0:T(8,128)(2,1)S(1)} %get-tuple-element.26), channel_id=1, source_target_pairs={{0,1},{1,0},{2,3},{3,2},{4,5},{5,4},{6,7},{7,6},{8,9},{9,8},{10,11... | collective-permute-start | bytes 393224 | tf_op jit(solution)/shard_map/ppermute | solution.py:24
  11.3 3.2 %constant_dynamic-slice_fusion.1 = bf16[256,4096]{1,0:T(8,128)(2,1)} fusion(bf16[256,8192]{1,0:T(8,128)(2,1)} %directions.3, s32[]{:T(128)S(6)} %select_n.13), kind=kLoop, calls=%fused_computation.4 | loop fusion | bytes 4194308 | tf_op jit(solution)/shard_map/dynamic_slice | solution.py:251
  14.4 0.0 collective-permute-done.1
  14.5 0.0 collective-permute-done
  14.5 0.1 copy.7
  14.6 1.1 broadcast_in_dim.6
  15.7 13.0 %all-to-all-start = ((bf16[16,128,256]{2,1,0:T(8,128)(2,1)}), bf16[16,128,256]{2,1,0:T(8,128)(2,1)S(1)}, u32[]{:S(2)}, u32[]{:S(2)}) async-start(bf16[16,128,256]{2,1,0:T(8,128)(2,1)} %broadcast_in_dim.6), calls=%async_computation | async-start | bytes 2097152 | tf_op jit(solution)/shard_map/all_to_all | solution.py:16
  28.7 2.2 %collective-permute-start.2 = (bf16[256,4096]{1,0:T(8,128)(2,1)}, bf16[256,4096]{1,0:T(8,128)(2,1)S(1)}, u32[]{:S(2)}, u32[]{:S(2)}) collective-permute-start(bf16[256,4096]{1,0:T(8,128)(2,1)} %constant_dynamic-slice_fusion.1), channel_id=1, source_target_pairs={{0,1},{1,0},{2,3},{3,2},{4,5},{5,4},{6,7},{7,6},{8,9},{9,8},{10,11... | collective-permute-start | bytes 6291464 | tf_op jit(solution)/shard_map/ppermute | solution.py:24
  30.9 3.2 %collective-permute-start.3 = (bf16[2,256,256]{2,1,0:T(8,128)(2,1)S(1)}, bf16[2,256,256]{2,1,0:T(8,128)(2,1)}, u32[]{:S(2)}, u32[]{:S(2)}) collective-permute-start(bf16[2,256,256]{2,1,0:T(8,128)(2,1)S(1)} %pad_maximum_fusion.refs_0_), channel_id=1, source_target_pairs={{0,128},{128,256},{256,384},{384,0},{1,129},{129,257},{257,385},{3... | collective-permute-start | bytes 786440 | tf_op jit(solution)/shard_map/ppermute | solution.py:24
  34.1 4.5 %collective-permute-start.4 = (bf16[2,256,256]{2,1,0:T(8,128)(2,1)S(1)}, bf16[2,256,256]{2,1,0:T(8,128)(2,1)}, u32[]{:S(2)}, u32[]{:S(2)}) collective-permute-start(bf16[2,256,256]{2,1,0:T(8,128)(2,1)S(1)} %pad_maximum_fusion.refs_0_), channel_id=1, source_target_pairs={{0,256},{128,384},{256,0},{384,128},{1,257},{129,385},{257,1},{385... | collective-permute-start | bytes 786440 | tf_op jit(solution)/shard_map/ppermute | solution.py:24
  38.6 3.0 %collective-permute-start.5 = (bf16[2,256,256]{2,1,0:T(8,128)(2,1)S(1)}, bf16[2,256,256]{2,1,0:T(8,128)(2,1)}, u32[]{:S(2)}, u32[]{:S(2)}) collective-permute-start(bf16[2,256,256]{2,1,0:T(8,128)(2,1)S(1)} %pad_maximum_fusion.refs_0_), channel_id=1, source_target_pairs={{0,384},{128,0},{256,128},{384,256},{1,385},{129,1},{257,129},{385... | collective-permute-start | bytes 786440 | tf_op jit(solution)/shard_map/ppermute | solution.py:24
  41.6 0.3 collective-permute-done.3.refs_1_
  41.9 6.7 %collective-permute-done.4.refs_2_ = bf16[2,256,256]{2,1,0:T(8,128)(2,1)} collective-permute-done((bf16[2,256,256]{2,1,0:T(8,128)(2,1)S(1)}, bf16[2,256,256]{2,1,0:T(8,128)(2,1)}, u32[]{:S(2)}, u32[]{:S(2)}) %collective-permute-start.4) | collective-permute-done | bytes 262176 | tf_op jit(solution)/shard_map/ppermute | solution.py:24
  48.6 1.1 collective-permute-done.5.refs_3_
  49.7 6.3 %all-to-all-done = bf16[16,128,256]{2,1,0:T(8,128)(2,1)S(1)} async-done(((bf16[16,128,256]{2,1,0:T(8,128)(2,1)}), bf16[16,128,256]{2,1,0:T(8,128)(2,1)S(1)}, u32[]{:S(2)}, u32[]{:S(2)}) %all-to-all-start) | async-done | bytes 1048608 | tf_op jit(solution)/shard_map/all_to_all | solution.py:16
  56.0 1.5 shard_map.65
  57.5 3.3 %collective-permute-start.6 = (f32[512,256]{1,0:T(8,128)S(1)}, f32[512,256]{1,0:T(8,128)S(1)}, u32[]{:S(2)}, u32[]{:S(2)}) collective-permute-start(f32[512,256]{1,0:T(8,128)S(1)} %shard_map.65), channel_id=1, source_target_pairs={{0,1},{1,0},{2,3},{3,2},{4,5},{5,4},{6,7},{7,6},{8,9},{9,8},{10,11... | collective-permute-start | bytes 1572872 | tf_op jit(solution)/shard_map/ppermute | solution.py:24
  60.9 1.5 shard_map.64.kept
  62.4 0.0 copy-start
  62.4 0.0 collective-permute-done.6.received
  62.4 0.2 shard_map.66
  62.7 23.1 %all_to_all.30 = f16[4,136,256]{2,1,0:T(8,128)(2,1)S(1)} all-to-all(f16[4,136,256]{2,1,0:T(8,128)(2,1)S(1)} %convert_element_type.6), channel_id=1, replica_groups=mesh['y'=4,'zh'=4,'x'=4,'zl'=4,'core'=2] {'zh'}, dimensions={0} | all-to-all | bytes 557056 | tf_op jit(solution)/shard_map/all_to_all | solution.py:16
  85.8 0.1 shard_map.67
  85.9 2.7 %all-gather = bf16[256,256]{1,0:T(8,128)(2,1)S(1)} all-gather(bf16[128,256]{1,0:T(8,128)(2,1)S(1)} %shard_map.67), channel_id=2, replica_groups=mesh['y'=4,'zh'=4,'x'=4,'zl'=4,'core'=2] {'core'}, dimensions={0}, use_global_device_ids=true | all-gather | bytes 196608 | tf_op jit(solution)/shard_map/all_gather | solution.py:269
  88.7 0.0 collective-permute-done.2.their_directions
  88.7 0.0 copy-done
  88.7 1.6 %shard_map.68 = bf16[4,4,128,256]{3,2,1,0:T(8,128)(2,1)S(1)} custom-call(s32[1]{0:T(128)} %bitcast.half, bf16[2,128,256]{2,1,0:T(8,128)(2,1)S(1)} %bitcast.18, bf16[256,8192]{1,0:T(8,128)(2,1)S(1)} %copy-done, bf16[256,4096]{1,0:T(8,128)(2,1)S(1)} %collective-permute-done.2.their_directions), custom_call_target="tpu_custom_call" | custom-call | flops 536870912 | bytes 4194304 | tf_op jit(solution)/shard_map/pallas_call | solution.py:127
  90.3 0.0 copy-start.2
  90.3 0.0 copy-start.3
  90.3 0.0 copy-start.4
  90.3 17.2 %all_to_all.31.parts = bf16[4,4,128,256]{3,2,1,0:T(8,128)(2,1)S(1)} all-to-all(bf16[4,4,128,256]{3,2,1,0:T(8,128)(2,1)S(1)} %shard_map.68), channel_id=1, replica_groups=mesh['y'=4,'zh'=4,'x'=4,'zl'=4,'core'=2] {'x'}, dimensions={0} | all-to-all | bytes 2097152 | tf_op jit(solution)/shard_map/all_to_all | solution.py:16
  107.6 0.8 shard_map.69
  108.4 4.2 %all-to-all-start.3 = ((bf16[4,128,256]{2,1,0:T(8,128)(2,1)}), bf16[4,128,256]{2,1,0:T(8,128)(2,1)S(1)}, u32[]{:S(2)}, u32[]{:S(2)}) async-start(bf16[4,128,256]{2,1,0:T(8,128)(2,1)} %shard_map.69), calls=%async_computation.3 | async-start | bytes 524288 | tf_op jit(solution)/shard_map/all_to_all | solution.py:16
  112.6 5.7 %all-to-all-done.3.parts = bf16[4,128,256]{2,1,0:T(8,128)(2,1)S(1)} async-done(((bf16[4,128,256]{2,1,0:T(8,128)(2,1)}), bf16[4,128,256]{2,1,0:T(8,128)(2,1)S(1)}, u32[]{:S(2)}, u32[]{:S(2)}) %all-to-all-start.3) | async-done | bytes 262176 | tf_op jit(solution)/shard_map/all_to_all | solution.py:16
  118.2 0.0 copy-done.2
  118.2 0.0 copy-done.3
  118.2 0.0 copy-done.4
  118.2 0.7 shard_map.70
  119.0 10.6 %all_to_all.32 = bf16[4,256,128]{2,1,0:T(8,128)(2,1)S(1)} all-to-all(bf16[4,256,128]{2,1,0:T(8,128)(2,1)S(1)} %broadcast_in_dim.7), channel_id=1, replica_groups=mesh['y'=4,'zh'=4,'x'=4,'zl'=4,'core'=2] {'zl'}, dimensions={0} | all-to-all | bytes 524288 | tf_op jit(solution)/shard_map/all_to_all | solution.py:16
  129.6 1.2 broadcast_in_dim.8
  130.8 3.5 %all-to-all-start.5 = ((bf16[4,4,256,128]{3,2,1,0:T(8,128)(2,1)}), bf16[4,4,256,128]{3,2,1,0:T(8,128)(2,1)S(1)}, u32[]{:S(2)}, u32[]{:S(2)}) async-start(bf16[4,4,256,128]{3,2,1,0:T(8,128)(2,1)} %broadcast_in_dim.8), calls=%async_computation.5 | async-start | bytes 2097152 | tf_op jit(solution)/shard_map/all_to_all | solution.py:16
  134.3 10.9 %all-to-all-done.5 = bf16[4,4,256,128]{3,2,1,0:T(8,128)(2,1)S(1)} async-done(((bf16[4,4,256,128]{3,2,1,0:T(8,128)(2,1)}), bf16[4,4,256,128]{3,2,1,0:T(8,128)(2,1)S(1)}, u32[]{:S(2)}, u32[]{:S(2)}) %all-to-all-start.5) | async-done | bytes 1048608 | tf_op jit(solution)/shard_map/all_to_all | solution.py:16
  145.2 0.0 copy-start.1
  145.2 2.2 %copy-done.1 = bf16[256,8192]{1,0:T(8,128)(2,1)S(1)} copy-done((bf16[256,8192]{1,0:T(8,128)(2,1)S(1)}, bf16[256,8192]{1,0:T(8,128)(2,1)}, u32[]{:S(2)}) %copy-start.1) | copy-done | bytes 4194328
  147.4 2.1 %shard_map.71 = (f32[256,128]{1,0:T(8,128)S(1)}, f32[256,128]{1,0:T(8,128)S(1)}) custom-call(s32[1]{0:T(128)} %bitcast.half, bf16[256,8192]{1,0:T(8,128)(2,1)S(1)} %copy-done.1, bf16[256,4096]{1,0:T(8,128)(2,1)S(1)} %collective-permute-done.2.their_directions, bf16[4096,128]{1,0:T(8,128)(2,1)S(1)} %bitcast.17), custom_call_target="tpu_custom_call" | custom-call | flops 536870912 | bytes 4194304 | tf_op jit(solution)/shard_map/pallas_call | solution.py:215
  149.5 6.8 %all-gather.1 = f32[512,128]{1,0:T(8,128)S(1)} all-gather(f32[256,128]{1,0:T(8,128)S(1)} %get-tuple-element.24), channel_id=3, replica_groups=mesh['y'=4,'zh'=4,'x'=4,'zl'=4,'core'=2] {'core'}, dimensions={0}, use_global_device_ids=true | all-gather | bytes 393216 | tf_op jit(solution)/shard_map/all_gather | solution.py:281
  156.3 0.7 bitcast_add_fusion
  (4 shorter events, 0.1 us)
Async XLA Ops:
  0.0 14.5 %collective-permute-start = (bf16[128,256]{0,1:T(8,128)(2,1)}, bf16[128,256]{0,1:T(8,128)(2,1)S(1)}, u32[]{:S(2)}, u32[]{:S(2)}) collective-permute-start(bf16[128,256]{0,1:T(8,128)(2,1)} %bitcast.23), channel_id=1, source_target_pairs={{0,0},{2,32},{4,64},{6,96},{32,2},{34,34},{36,66},{38,98},{64,4},{... | collective-permute-start | bytes 196616 | tf_op jit(solution)/shard_map/ppermute | solution.py:250
  2.5 12.0 %collective-permute-start.1 = (bf16[256,256]{1,0:T(8,128)(2,1)S(1)}, bf16[256,256]{1,0:T(8,128)(2,1)S(1)}, u32[]{:S(2)}, u32[]{:S(2)}) collective-permute-start(bf16[256,256]{1,0:T(8,128)(2,1)S(1)} %get-tuple-element.26), channel_id=1, source_target_pairs={{0,1},{1,0},{2,3},{3,2},{4,5},{5,4},{6,7},{7,6},{8,9},{9,8},{10,11... | collective-permute-start | bytes 393224 | tf_op jit(solution)/shard_map/ppermute | solution.py:24
  15.7 40.3 %all-to-all-start = ((bf16[16,128,256]{2,1,0:T(8,128)(2,1)}), bf16[16,128,256]{2,1,0:T(8,128)(2,1)S(1)}, u32[]{:S(2)}, u32[]{:S(2)}) async-start(bf16[16,128,256]{2,1,0:T(8,128)(2,1)} %broadcast_in_dim.6), calls=%async_computation | async-start | bytes 2097152 | tf_op jit(solution)/shard_map/all_to_all | solution.py:16
  28.7 60.0 %collective-permute-start.2 = (bf16[256,4096]{1,0:T(8,128)(2,1)}, bf16[256,4096]{1,0:T(8,128)(2,1)S(1)}, u32[]{:S(2)}, u32[]{:S(2)}) collective-permute-start(bf16[256,4096]{1,0:T(8,128)(2,1)} %constant_dynamic-slice_fusion.1), channel_id=1, source_target_pairs={{0,1},{1,0},{2,3},{3,2},{4,5},{5,4},{6,7},{7,6},{8,9},{9,8},{10,11... | collective-permute-start | bytes 6291464 | tf_op jit(solution)/shard_map/ppermute | solution.py:24
  30.9 11.1 %collective-permute-start.3 = (bf16[2,256,256]{2,1,0:T(8,128)(2,1)S(1)}, bf16[2,256,256]{2,1,0:T(8,128)(2,1)}, u32[]{:S(2)}, u32[]{:S(2)}) collective-permute-start(bf16[2,256,256]{2,1,0:T(8,128)(2,1)S(1)} %pad_maximum_fusion.refs_0_), channel_id=1, source_target_pairs={{0,128},{128,256},{256,384},{384,0},{1,129},{129,257},{257,385},{3... | collective-permute-start | bytes 786440 | tf_op jit(solution)/shard_map/ppermute | solution.py:24
  34.1 14.6 %collective-permute-start.4 = (bf16[2,256,256]{2,1,0:T(8,128)(2,1)S(1)}, bf16[2,256,256]{2,1,0:T(8,128)(2,1)}, u32[]{:S(2)}, u32[]{:S(2)}) collective-permute-start(bf16[2,256,256]{2,1,0:T(8,128)(2,1)S(1)} %pad_maximum_fusion.refs_0_), channel_id=1, source_target_pairs={{0,256},{128,384},{256,0},{384,128},{1,257},{129,385},{257,1},{385... | collective-permute-start | bytes 786440 | tf_op jit(solution)/shard_map/ppermute | solution.py:24
  38.6 11.1 %collective-permute-start.5 = (bf16[2,256,256]{2,1,0:T(8,128)(2,1)S(1)}, bf16[2,256,256]{2,1,0:T(8,128)(2,1)}, u32[]{:S(2)}, u32[]{:S(2)}) collective-permute-start(bf16[2,256,256]{2,1,0:T(8,128)(2,1)S(1)} %pad_maximum_fusion.refs_0_), channel_id=1, source_target_pairs={{0,384},{128,0},{256,128},{384,256},{1,385},{129,1},{257,129},{385... | collective-permute-start | bytes 786440 | tf_op jit(solution)/shard_map/ppermute | solution.py:24
  57.5 4.9 %collective-permute-start.6 = (f32[512,256]{1,0:T(8,128)S(1)}, f32[512,256]{1,0:T(8,128)S(1)}, u32[]{:S(2)}, u32[]{:S(2)}) collective-permute-start(f32[512,256]{1,0:T(8,128)S(1)} %shard_map.65), channel_id=1, source_target_pairs={{0,1},{1,0},{2,3},{3,2},{4,5},{5,4},{6,7},{7,6},{8,9},{9,8},{10,11... | collective-permute-start | bytes 1572872 | tf_op jit(solution)/shard_map/ppermute | solution.py:24
  62.4 26.2 %copy-start = (bf16[256,8192]{1,0:T(8,128)(2,1)S(1)}, bf16[256,8192]{1,0:T(8,128)(2,1)}, u32[]{:S(2)}) copy-start(bf16[256,8192]{1,0:T(8,128)(2,1)} %directions.3) | copy-start | bytes 12582916
  90.3 28.0 %copy-start.2 = (f32[8192]{0:T(1024)S(1)}, f32[8192]{0:T(1024)}, u32[]{:S(2)}) copy-start(f32[8192]{0:T(1024)} %param.9) | copy-start | bytes 98308
  90.3 28.0 %copy-start.3 = (s32[128]{0:T(128)S(1)}, s32[128]{0:T(128)}, u32[]{:S(2)}) copy-start(s32[128]{0:T(128)} %param.11) | copy-start | bytes 1540
  90.3 27.9 %copy-start.4 = (f32[16]{0:T(128)S(1)}, f32[16]{0:T(128)}, u32[]{:S(2)}) copy-start(f32[16]{0:T(128)} %grid_values.1) | copy-start | bytes 196
  108.4 9.9 %all-to-all-start.3 = ((bf16[4,128,256]{2,1,0:T(8,128)(2,1)}), bf16[4,128,256]{2,1,0:T(8,128)(2,1)S(1)}, u32[]{:S(2)}, u32[]{:S(2)}) async-start(bf16[4,128,256]{2,1,0:T(8,128)(2,1)} %shard_map.69), calls=%async_computation.3 | async-start | bytes 524288 | tf_op jit(solution)/shard_map/all_to_all | solution.py:16
  130.8 14.4 %all-to-all-start.5 = ((bf16[4,4,256,128]{3,2,1,0:T(8,128)(2,1)}), bf16[4,4,256,128]{3,2,1,0:T(8,128)(2,1)S(1)}, u32[]{:S(2)}, u32[]{:S(2)}) async-start(bf16[4,4,256,128]{3,2,1,0:T(8,128)(2,1)} %broadcast_in_dim.8), calls=%async_computation.5 | async-start | bytes 2097152 | tf_op jit(solution)/shard_map/all_to_all | solution.py:16
  145.2 2.2 %copy-start.1 = (bf16[256,8192]{1,0:T(8,128)(2,1)S(1)}, bf16[256,8192]{1,0:T(8,128)(2,1)}, u32[]{:S(2)}) copy-start(bf16[256,8192]{1,0:T(8,128)(2,1)} %directions.3) | copy-start | bytes 12582916

commit v7 on v5

--- a/solution.py
+++ b/solution.py
@@ -197,20 +197,24 @@
     )(which, parts, strengths.reshape(-1, 1, share), slots.reshape(1, voxels), grid_values)
 
 
-def encode_kernel(half, directions, shrunk, out):
+def encode_kernel(first, half, directions, shrunk, *refs):
+    out = refs[-1]
+
     @pl.when(pl.program_id(0) == 0)
     def _():
-        out[...] = jnp.zeros_like(out)
+        out[...] = jnp.zeros_like(out) if first else refs[0][...]
 
     out[...] += jnp.dot(directions[...], shrunk[...], preferred_element_type=F32)
 
 
-def encode(half, directions, shrunk, steps=4):
+def encode(half, directions, shrunk, total=None, steps=4):
     rows, _ = directions.shape
     depth, voxels = shrunk.shape
     columns = depth // steps
-    return pl.pallas_call(
-        encode_kernel,
+    first = total is None
+    flat = pl.BlockSpec((rows, voxels), lambda i, h: (0, 0))
+    return pl.pallas_call(
+        functools.partial(encode_kernel, first),
         out_shape=jax.ShapeDtypeStruct((rows, voxels), F32),
         grid_spec=pltpu.PrefetchScalarGridSpec(
             num_scalar_prefetch=1,
@@ -218,14 +222,15 @@
             in_specs=[
                 pl.BlockSpec((rows, columns), lambda i, h: (0, h[0] * steps + i)),
                 pl.BlockSpec((columns, voxels), lambda i, h: (i, 0)),
-            ],
-            out_specs=pl.BlockSpec((rows, voxels), lambda i, h: (0, 0)),
+            ]
+            + ([] if first else [flat]),
+            out_specs=flat,
         ),
         compiler_params=pltpu.CompilerParams(vmem_limit_bytes=16 << 20),
         cost_estimate=pl.CostEstimate(
             flops=2 * rows * depth * voxels, bytes_accessed=4 << 20, transcendentals=0
         ),
-    )(half, directions, shrunk)
+    )(half, directions, shrunk, *([] if first else [total]))
 
 
 def per_device(
@@ -275,7 +280,7 @@
     shrunk = gather(shrunk, "x", nx).reshape(width // 2, -1)
     theirs = encode(jnp.zeros((1,), jnp.int32), their_directions, shrunk)
     received = shift(theirs, "core", 2, 1)
-    return encode(mine, spectral_directions, shrunk) + received
+    return encode(mine, spectral_directions, shrunk, received)
 
 
 def solution(mesh):

time: 155 us -> 156 us (level)
  transfers between devices with their start and end apart: 10 -> 10, of which waited for: 5 -> 6; matrix products, arithmetic and copies ran while one was open for 3% -> 3% of each run, Pallas kernels for 3% -> 2%
where the time goes in v7:
time: 156 us; the launch traced here: 155 us
  blocking collectives  67.6 us (43%)
  starting transfers between devices  50.4 us (32%)
  waiting for transfers between devices  21 us (13%)
  Pallas kernels  9.92 us (6%)
  local copies, waits for them, and re-layouts  5.58 us (4%)
    all_to_all x4, blocking collectives, exchange(): return lax.all_to_all(blocks, axis, 0, 0, tiled=True)  64.8 us
    ppermute x7, starting transfers between devices, shift(): lax.ppermute(block, axis, [(i, (i + by) % size) for i in range(size)])  31.8 us
    all_to_all x2, starting transfers between devices, exchange(): return lax.all_to_all(blocks, axis, 0, 0, tiled=True)  17.2 us
    all_to_all x2, waiting for transfers between devices, exchange(): return lax.all_to_all(blocks, axis, 0, 0, tiled=True)  12 us
    ppermute x7, waiting for transfers between devices, shift(): lax.ppermute(block, axis, [(i, (i + by) % size) for i in range(size)])  9.08 us
    pallas_call x2, Pallas kernels, encode(): pl.pallas_call(functools.partial(encode_kernel, first), out_shape=jax.Sha...  3.41 us
    dynamic_slice x1, local copies, waits for them, and re-layouts, per_device(): lax.dynamic_slice_in_dim(spectral_directions, (1 - core) * (width // 2),...  3.16 us
  transfers between devices with their start and end apart: 10, of which 6 were waited for; matrix products, arithmetic and copies ran while one was open for 3% of the time, Pallas kernels for 2%

profile of v7, /device:TPU:1, one launch (start us, length us, event | category | flops | bytes accessed | tf_op | source)
XLA Modules:
  0.0 154.9 jit_solution(9676575550100865747)
XLA Ops:
  0.0 1.5 collective-permute-start
  1.5 1.0 dynamic-slice_bitcast_fusion
  2.5 8.8 %collective-permute-start.1 = (bf16[256,256]{1,0:T(8,128)(2,1)S(1)}, bf16[256,256]{1,0:T(8,128)(2,1)S(1)}, u32[]{:S(2)}, u32[]{:S(2)}) collective-permute-start(bf16[256,256]{1,0:T(8,128)(2,1)S(1)} %get-tuple-element.22), channel_id=1, source_target_pairs={{0,1},{1,0},{2,3},{3,2},{4,5},{5,4},{6,7},{7,6},{8,9},{9,8},{10,11... | collective-permute-start | bytes 393224 | tf_op jit(solution)/shard_map/ppermute | solution.py:24
  11.3 3.2 %constant_dynamic-slice_fusion.1 = bf16[256,4096]{1,0:T(8,128)(2,1)} fusion(bf16[256,8192]{1,0:T(8,128)(2,1)} %directions.3, s32[]{:T(128)S(6)} %select_n.9), kind=kLoop, calls=%fused_computation.3 | loop fusion | bytes 4194308 | tf_op jit(solution)/shard_map/dynamic_slice | solution.py:252
  14.4 0.0 collective-permute-done.1
  14.5 0.0 collective-permute-done
  14.5 0.1 copy.7
  14.6 1.1 broadcast_in_dim.6
  15.7 13.0 %all-to-all-start = ((bf16[16,128,256]{2,1,0:T(8,128)(2,1)}), bf16[16,128,256]{2,1,0:T(8,128)(2,1)S(1)}, u32[]{:S(2)}, u32[]{:S(2)}) async-start(bf16[16,128,256]{2,1,0:T(8,128)(2,1)} %broadcast_in_dim.6), calls=%async_computation | async-start | bytes 2097152 | tf_op jit(solution)/shard_map/all_to_all | solution.py:16
  28.7 2.2 %collective-permute-start.6 = (bf16[256,4096]{1,0:T(8,128)(2,1)}, bf16[256,4096]{1,0:T(8,128)(2,1)S(1)}, u32[]{:S(2)}, u32[]{:S(2)}) collective-permute-start(bf16[256,4096]{1,0:T(8,128)(2,1)} %constant_dynamic-slice_fusion.1), channel_id=1, source_target_pairs={{0,1},{1,0},{2,3},{3,2},{4,5},{5,4},{6,7},{7,6},{8,9},{9,8},{10,11... | collective-permute-start | bytes 6291464 | tf_op jit(solution)/shard_map/ppermute | solution.py:24
  30.9 3.2 %collective-permute-start.2 = (bf16[2,256,256]{2,1,0:T(8,128)(2,1)S(1)}, bf16[2,256,256]{2,1,0:T(8,128)(2,1)}, u32[]{:S(2)}, u32[]{:S(2)}) collective-permute-start(bf16[2,256,256]{2,1,0:T(8,128)(2,1)S(1)} %pad_maximum_fusion.refs_0_), channel_id=1, source_target_pairs={{0,128},{128,256},{256,384},{384,0},{1,129},{129,257},{257,385},{3... | collective-permute-start | bytes 786440 | tf_op jit(solution)/shard_map/ppermute | solution.py:24
  34.1 4.5 %collective-permute-start.3 = (bf16[2,256,256]{2,1,0:T(8,128)(2,1)S(1)}, bf16[2,256,256]{2,1,0:T(8,128)(2,1)}, u32[]{:S(2)}, u32[]{:S(2)}) collective-permute-start(bf16[2,256,256]{2,1,0:T(8,128)(2,1)S(1)} %pad_maximum_fusion.refs_0_), channel_id=1, source_target_pairs={{0,256},{128,384},{256,0},{384,128},{1,257},{129,385},{257,1},{385... | collective-permute-start | bytes 786440 | tf_op jit(solution)/shard_map/ppermute | solution.py:24
  38.6 3.0 %collective-permute-start.4 = (bf16[2,256,256]{2,1,0:T(8,128)(2,1)S(1)}, bf16[2,256,256]{2,1,0:T(8,128)(2,1)}, u32[]{:S(2)}, u32[]{:S(2)}) collective-permute-start(bf16[2,256,256]{2,1,0:T(8,128)(2,1)S(1)} %pad_maximum_fusion.refs_0_), channel_id=1, source_target_pairs={{0,384},{128,0},{256,128},{384,256},{1,385},{129,1},{257,129},{385... | collective-permute-start | bytes 786440 | tf_op jit(solution)/shard_map/ppermute | solution.py:24
  41.6 0.3 collective-permute-done.2.refs_1_
  41.9 6.7 %collective-permute-done.3.refs_2_ = bf16[2,256,256]{2,1,0:T(8,128)(2,1)} collective-permute-done((bf16[2,256,256]{2,1,0:T(8,128)(2,1)S(1)}, bf16[2,256,256]{2,1,0:T(8,128)(2,1)}, u32[]{:S(2)}, u32[]{:S(2)}) %collective-permute-start.3) | collective-permute-done | bytes 262176 | tf_op jit(solution)/shard_map/ppermute | solution.py:24
  48.6 1.1 collective-permute-done.4.refs_3_
  49.7 6.3 %all-to-all-done = bf16[16,128,256]{2,1,0:T(8,128)(2,1)S(1)} async-done(((bf16[16,128,256]{2,1,0:T(8,128)(2,1)}), bf16[16,128,256]{2,1,0:T(8,128)(2,1)S(1)}, u32[]{:S(2)}, u32[]{:S(2)}) %all-to-all-start) | async-done | bytes 1048608 | tf_op jit(solution)/shard_map/all_to_all | solution.py:16
  56.0 1.5 shard_map.65
  57.5 3.3 %collective-permute-start.5 = (f32[512,256]{1,0:T(8,128)S(1)}, f32[512,256]{1,0:T(8,128)S(1)}, u32[]{:S(2)}, u32[]{:S(2)}) collective-permute-start(f32[512,256]{1,0:T(8,128)S(1)} %shard_map.65), channel_id=1, source_target_pairs={{0,1},{1,0},{2,3},{3,2},{4,5},{5,4},{6,7},{7,6},{8,9},{9,8},{10,11... | collective-permute-start | bytes 1572872 | tf_op jit(solution)/shard_map/ppermute | solution.py:24
  60.9 1.5 shard_map.64.kept
  62.4 0.0 copy-start
  62.4 0.0 collective-permute-done.5.received
  62.4 0.2 shard_map.66
  62.7 23.1 %all_to_all.30 = f16[4,136,256]{2,1,0:T(8,128)(2,1)S(1)} all-to-all(f16[4,136,256]{2,1,0:T(8,128)(2,1)S(1)} %convert_element_type.6), channel_id=1, replica_groups=mesh['y'=4,'zh'=4,'x'=4,'zl'=4,'core'=2] {'zh'}, dimensions={0} | all-to-all | bytes 557056 | tf_op jit(solution)/shard_map/all_to_all | solution.py:16
  85.8 0.1 shard_map.67
  85.9 2.7 %all-gather = bf16[256,256]{1,0:T(8,128)(2,1)S(1)} all-gather(bf16[128,256]{1,0:T(8,128)(2,1)S(1)} %shard_map.67), channel_id=2, replica_groups=mesh['y'=4,'zh'=4,'x'=4,'zl'=4,'core'=2] {'core'}, dimensions={0}, use_global_device_ids=true | all-gather | bytes 196608 | tf_op jit(solution)/shard_map/all_gather | solution.py:270
  88.6 0.0 collective-permute-done.6.their_directions.directions
  88.6 0.0 copy-done
  88.6 1.6 %shard_map.68 = bf16[4,4,128,256]{3,2,1,0:T(8,128)(2,1)S(1)} custom-call(s32[1]{0:T(128)} %bitcast.half, bf16[2,128,256]{2,1,0:T(8,128)(2,1)S(1)} %bitcast.16, bf16[256,8192]{1,0:T(8,128)(2,1)S(1)} %copy-done, bf16[256,4096]{1,0:T(8,128)(2,1)S(1)} %collective-permute-done.6.their_directions.directions), custom_call_target="tpu_custom_call" | custom-call | flops 536870912 | bytes 4194304 | tf_op jit(solution)/shard_map/pallas_call | solution.py:127
  90.3 0.0 copy-start.2
  90.3 0.0 copy-start.3
  90.3 0.0 copy-start.4
  90.3 17.2 %all_to_all.31.parts = bf16[4,4,128,256]{3,2,1,0:T(8,128)(2,1)S(1)} all-to-all(bf16[4,4,128,256]{3,2,1,0:T(8,128)(2,1)S(1)} %shard_map.68), channel_id=1, replica_groups=mesh['y'=4,'zh'=4,'x'=4,'zl'=4,'core'=2] {'x'}, dimensions={0} | all-to-all | bytes 2097152 | tf_op jit(solution)/shard_map/all_to_all | solution.py:16
  107.5 0.8 shard_map.69
  108.4 4.2 %all-to-all-start.3 = ((bf16[4,128,256]{2,1,0:T(8,128)(2,1)}), bf16[4,128,256]{2,1,0:T(8,128)(2,1)S(1)}, u32[]{:S(2)}, u32[]{:S(2)}) async-start(bf16[4,128,256]{2,1,0:T(8,128)(2,1)} %shard_map.69), calls=%async_computation.3 | async-start | bytes 524288 | tf_op jit(solution)/shard_map/all_to_all | solution.py:16
  112.6 5.7 %all-to-all-done.3.parts = bf16[4,128,256]{2,1,0:T(8,128)(2,1)S(1)} async-done(((bf16[4,128,256]{2,1,0:T(8,128)(2,1)}), bf16[4,128,256]{2,1,0:T(8,128)(2,1)S(1)}, u32[]{:S(2)}, u32[]{:S(2)}) %all-to-all-start.3) | async-done | bytes 262176 | tf_op jit(solution)/shard_map/all_to_all | solution.py:16
  118.2 0.0 copy-done.2
  118.2 0.0 copy-done.3
  118.2 0.0 copy-done.4
  118.2 0.7 shard_map.70
  119.0 10.6 %all_to_all.32 = bf16[4,256,128]{2,1,0:T(8,128)(2,1)S(1)} all-to-all(bf16[4,256,128]{2,1,0:T(8,128)(2,1)S(1)} %broadcast_in_dim.7), channel_id=1, replica_groups=mesh['y'=4,'zh'=4,'x'=4,'zl'=4,'core'=2] {'zl'}, dimensions={0} | all-to-all | bytes 524288 | tf_op jit(solution)/shard_map/all_to_all | solution.py:16
  129.6 0.2 broadcast_in_dim.8
  129.8 0.0 copy-start.1
  129.8 13.9 %all_to_all.33 = bf16[4,4,256,128]{3,2,1,0:T(8,128)(2,1)S(1)} all-to-all(bf16[4,4,256,128]{3,2,1,0:T(8,128)(2,1)S(1)} %broadcast_in_dim.8), channel_id=1, replica_groups=mesh['y'=4,'zh'=4,'x'=4,'zl'=4,'core'=2] {'x'}, dimensions={0} | all-to-all | bytes 2097152 | tf_op jit(solution)/shard_map/all_to_all | solution.py:16
  143.7 1.4 shard_map.71
  145.1 6.8 %collective-permute-start.7 = (f32[256,128]{1,0:T(8,128)S(1)}, f32[256,128]{1,0:T(8,128)S(1)}, u32[]{:S(2)}, u32[]{:S(2)}) collective-permute-start(f32[256,128]{1,0:T(8,128)S(1)} %shard_map.71), channel_id=1, source_target_pairs={{0,1},{1,0},{2,3},{3,2},{4,5},{5,4},{6,7},{7,6},{8,9},{9,8},{10,11... | collective-permute-start | bytes 393224 | tf_op jit(solution)/shard_map/ppermute | solution.py:24
  151.9 1.0 collective-permute-done.7.refs_0_
  152.8 0.0 copy-done.1
  152.8 2.0 %shard_map.72 = f32[256,128]{1,0:T(8,128)} custom-call(s32[1]{0:T(128)} %bitcast.half, bf16[256,8192]{1,0:T(8,128)(2,1)S(1)} %copy-done.1, bf16[4096,128]{1,0:T(8,128)(2,1)S(1)} %bitcast.15, f32[256,128]{1,0:T(8,128)S(1)} %collective-permute-done.7.refs_0_), custom_call_target="tpu_custom_call" | custom-call | flops 268435456 | bytes 4194304 | tf_op jit(solution)/shard_map/pallas_call | solution.py:216
  (4 shorter events, 0.1 us)
Async XLA Ops:
  0.0 14.5 %collective-permute-start = (bf16[128,256]{0,1:T(8,128)(2,1)}, bf16[128,256]{0,1:T(8,128)(2,1)S(1)}, u32[]{:S(2)}, u32[]{:S(2)}) collective-permute-start(bf16[128,256]{0,1:T(8,128)(2,1)} %bitcast.20), channel_id=1, source_target_pairs={{0,0},{2,32},{4,64},{6,96},{32,2},{34,34},{36,66},{38,98},{64,4},{... | collective-permute-start | bytes 196616 | tf_op jit(solution)/shard_map/ppermute | solution.py:251
  2.5 12.0 %collective-permute-start.1 = (bf16[256,256]{1,0:T(8,128)(2,1)S(1)}, bf16[256,256]{1,0:T(8,128)(2,1)S(1)}, u32[]{:S(2)}, u32[]{:S(2)}) collective-permute-start(bf16[256,256]{1,0:T(8,128)(2,1)S(1)} %get-tuple-element.22), channel_id=1, source_target_pairs={{0,1},{1,0},{2,3},{3,2},{4,5},{5,4},{6,7},{7,6},{8,9},{9,8},{10,11... | collective-permute-start | bytes 393224 | tf_op jit(solution)/shard_map/ppermute | solution.py:24
  15.7 40.3 %all-to-all-start = ((bf16[16,128,256]{2,1,0:T(8,128)(2,1)}), bf16[16,128,256]{2,1,0:T(8,128)(2,1)S(1)}, u32[]{:S(2)}, u32[]{:S(2)}) async-start(bf16[16,128,256]{2,1,0:T(8,128)(2,1)} %broadcast_in_dim.6), calls=%async_computation | async-start | bytes 2097152 | tf_op jit(solution)/shard_map/all_to_all | solution.py:16
  28.7 60.0 %collective-permute-start.6 = (bf16[256,4096]{1,0:T(8,128)(2,1)}, bf16[256,4096]{1,0:T(8,128)(2,1)S(1)}, u32[]{:S(2)}, u32[]{:S(2)}) collective-permute-start(bf16[256,4096]{1,0:T(8,128)(2,1)} %constant_dynamic-slice_fusion.1), channel_id=1, source_target_pairs={{0,1},{1,0},{2,3},{3,2},{4,5},{5,4},{6,7},{7,6},{8,9},{9,8},{10,11... | collective-permute-start | bytes 6291464 | tf_op jit(solution)/shard_map/ppermute | solution.py:24
  30.9 11.1 %collective-permute-start.2 = (bf16[2,256,256]{2,1,0:T(8,128)(2,1)S(1)}, bf16[2,256,256]{2,1,0:T(8,128)(2,1)}, u32[]{:S(2)}, u32[]{:S(2)}) collective-permute-start(bf16[2,256,256]{2,1,0:T(8,128)(2,1)S(1)} %pad_maximum_fusion.refs_0_), channel_id=1, source_target_pairs={{0,128},{128,256},{256,384},{384,0},{1,129},{129,257},{257,385},{3... | collective-permute-start | bytes 786440 | tf_op jit(solution)/shard_map/ppermute | solution.py:24
  34.1 14.6 %collective-permute-start.3 = (bf16[2,256,256]{2,1,0:T(8,128)(2,1)S(1)}, bf16[2,256,256]{2,1,0:T(8,128)(2,1)}, u32[]{:S(2)}, u32[]{:S(2)}) collective-permute-start(bf16[2,256,256]{2,1,0:T(8,128)(2,1)S(1)} %pad_maximum_fusion.refs_0_), channel_id=1, source_target_pairs={{0,256},{128,384},{256,0},{384,128},{1,257},{129,385},{257,1},{385... | collective-permute-start | bytes 786440 | tf_op jit(solution)/shard_map/ppermute | solution.py:24
  38.6 11.1 %collective-permute-start.4 = (bf16[2,256,256]{2,1,0:T(8,128)(2,1)S(1)}, bf16[2,256,256]{2,1,0:T(8,128)(2,1)}, u32[]{:S(2)}, u32[]{:S(2)}) collective-permute-start(bf16[2,256,256]{2,1,0:T(8,128)(2,1)S(1)} %pad_maximum_fusion.refs_0_), channel_id=1, source_target_pairs={{0,384},{128,0},{256,128},{384,256},{1,385},{129,1},{257,129},{385... | collective-permute-start | bytes 786440 | tf_op jit(solution)/shard_map/ppermute | solution.py:24
  57.5 4.9 %collective-permute-start.5 = (f32[512,256]{1,0:T(8,128)S(1)}, f32[512,256]{1,0:T(8,128)S(1)}, u32[]{:S(2)}, u32[]{:S(2)}) collective-permute-start(f32[512,256]{1,0:T(8,128)S(1)} %shard_map.65), channel_id=1, source_target_pairs={{0,1},{1,0},{2,3},{3,2},{4,5},{5,4},{6,7},{7,6},{8,9},{9,8},{10,11... | collective-permute-start | bytes 1572872 | tf_op jit(solution)/shard_map/ppermute | solution.py:24
  62.4 26.2 %copy-start = (bf16[256,8192]{1,0:T(8,128)(2,1)S(1)}, bf16[256,8192]{1,0:T(8,128)(2,1)}, u32[]{:S(2)}) copy-start(bf16[256,8192]{1,0:T(8,128)(2,1)} %directions.3) | copy-start | bytes 12582916
  90.3 28.0 %copy-start.2 = (f32[8192]{0:T(1024)S(1)}, f32[8192]{0:T(1024)}, u32[]{:S(2)}) copy-start(f32[8192]{0:T(1024)} %param.9) | copy-start | bytes 98308
  90.3 27.9 %copy-start.3 = (s32[128]{0:T(128)S(1)}, s32[128]{0:T(128)}, u32[]{:S(2)}) copy-start(s32[128]{0:T(128)} %param.11) | copy-start | bytes 1540
  90.3 27.9 %copy-start.4 = (f32[16]{0:T(128)S(1)}, f32[16]{0:T(128)}, u32[]{:S(2)}) copy-start(f32[16]{0:T(128)} %grid_values.1) | copy-start | bytes 196
  108.4 9.9 %all-to-all-start.3 = ((bf16[4,128,256]{2,1,0:T(8,128)(2,1)}), bf16[4,128,256]{2,1,0:T(8,128)(2,1)S(1)}, u32[]{:S(2)}, u32[]{:S(2)}) async-start(bf16[4,128,256]{2,1,0:T(8,128)(2,1)} %shard_map.69), calls=%async_computation.3 | async-start | bytes 524288 | tf_op jit(solution)/shard_map/all_to_all | solution.py:16
  129.8 23.0 %copy-start.1 = (bf16[256,8192]{1,0:T(8,128)(2,1)S(1)}, bf16[256,8192]{1,0:T(8,128)(2,1)}, u32[]{:S(2)}) copy-start(bf16[256,8192]{1,0:T(8,128)(2,1)} %directions.3) | copy-start | bytes 12582916
  145.1 7.7 %collective-permute-start.7 = (f32[256,128]{1,0:T(8,128)S(1)}, f32[256,128]{1,0:T(8,128)S(1)}, u32[]{:S(2)}, u32[]{:S(2)}) collective-permute-start(f32[256,128]{1,0:T(8,128)S(1)} %shard_map.71), channel_id=1, source_target_pairs={{0,1},{1,0},{2,3},{3,2},{4,5},{5,4},{6,7},{7,6},{8,9},{9,8},{10,11... | collective-permute-start | bytes 393224 | tf_op jit(solution)/shard_map/ppermute | solution.py:24
